TPU v7x, 128 devices: a whole 4x4x4 slice. The times are simulated.
128 devices in a mesh: seq: 64 (over y, z_lo, x, core), head: 2 (over z_hi).
Axes of the slice: x: 4, y: 4, z: 4 (z_hi: 2, z_lo: 2; z = z_hi * 2 + z_lo), core: 2. Of those that a mesh axis runs over, the one named last changes fastest.
Arguments:
- queries: bfloat16 [32768, 768], P('seq', 'head'), may hold values from -6 to 6
- keys: bfloat16 [32768, 768], P('seq', 'head'), may hold values from -6 to 6
- values: bfloat16 [32768, 768], P('seq', 'head'), may hold values from -6 to 6
- offsets: int32 [2, 12], replicated, may hold values from 0 to 63, as said below
- w_out: bfloat16 [768, 768], P('head'), may hold values from -0.21875 to 0.21875
- grad_mixed: bfloat16 [32768, 768], P('seq', 'head'), may hold values from -6 to 6
Outputs:
- mixed: bfloat16 [32768, 768], P('seq', 'head')
- grad_queries: bfloat16 [32768, 768], P('seq', 'head')
- grad_keys: bfloat16 [32768, 768], P('seq', 'head')
- grad_values: bfloat16 [32768, 768], P('seq', 'head')
- grad_w_out: float32 [768, 768], P('head')
Inputs may be any that keep to these rules, and one draw needn't show every extreme that they name: `offsets`: row 0 holds each head's offset at level 1, below 4; row 1 its offset at level 2, below 64.
All inputs are finite; a program needn't handle non-finite values.
Results may differ from a plain program's by a relative error of at most 0.023.
Values may be sent and summed in bfloat16 or wider, within the bound.
A program may use at most 128 MiB of HBM per device.

v0:
```python
import jax
import jax.numpy as jnp
from jax import lax
from jax.sharding import PartitionSpec as P

HD = 64
G_MID = 4


def as_sent(value):
    return jax.tree.map(lambda a: a.astype(jnp.bfloat16) if a.dtype == jnp.float32 else a, value)


def partner(value, axis, stride):
    mask = 2**stride
    pairs = [(source, source ^ mask) for source in range(lax.axis_size(axis))]
    return lax.ppermute(value, axis, pairs)


def hit_table(stride, offset):
    return jnp.arange(stride, dtype=jnp.int32)[:, None] == offset[None, :]


def pick_rows(source, stride, offset):
    trailing = source.shape[2:]
    grouped = source.reshape((source.shape[0] // stride, stride) + source.shape[1:])
    hits = hit_table(stride, offset).reshape((1, stride, source.shape[1]) + (1,) * len(trailing))
    return jnp.sum(jnp.where(hits, grouped, jnp.zeros((), source.dtype)), axis=1)


def put_rows(source, stride, offset):
    trailing = source.shape[2:]
    hits = hit_table(stride, offset).reshape((1, stride, source.shape[1]) + (1,) * len(trailing))
    spread = jnp.where(hits, source[:, None], jnp.zeros((), source.dtype))
    return spread.reshape((source.shape[0] * stride,) + source.shape[1:])


def to_heads(source):
    return jnp.moveaxis(source, 1, 0)


def from_heads(source):
    return jnp.moveaxis(source, 0, 1)


def head_scores(query_rows, key_rows):
    return jnp.einsum("qd,kd->qk", query_rows, key_rows, preferred_element_type=jnp.float32) * 0.125


def head_lse(inputs):
    query_rows, key_rows = inputs
    scores = head_scores(query_rows, key_rows)
    highest = jnp.max(scores, axis=1, keepdims=True)
    return highest[:, 0] + jnp.log(jnp.sum(jnp.exp(scores - highest), axis=1))


def head_out(inputs):
    query_rows, key_rows, value_rows, lse_rows = inputs
    weights_bf = jnp.exp(head_scores(query_rows, key_rows) - lse_rows[:, None]).astype(jnp.bfloat16)
    return jnp.einsum("qk,kd->qd", weights_bf, value_rows, preferred_element_type=jnp.float32)


def score_grads(query_rows, key_rows, value_rows, grad_rows, lse_rows, delta_rows):
    exact_probs = jnp.exp(head_scores(query_rows, key_rows) - lse_rows[:, None])
    grad_prob = jnp.einsum("qd,kd->qk", grad_rows, value_rows, preferred_element_type=jnp.float32)
    dscore = (0.125 * exact_probs * (grad_prob - delta_rows[:, None])).astype(jnp.bfloat16)
    return (exact_probs.astype(jnp.bfloat16), dscore)


def head_grads(inputs):
    query_rows, key_rows, value_rows, grad_rows, lse_rows, delta_rows = inputs
    weights_bf, dscore = score_grads(
        query_rows, key_rows, value_rows, grad_rows, lse_rows, delta_rows
    )
    grad_query = jnp.einsum("qk,kd->qd", dscore, key_rows, preferred_element_type=jnp.float32)
    grad_key = jnp.einsum("qk,qd->kd", dscore, query_rows, preferred_element_type=jnp.float32)
    grad_value = jnp.einsum("qk,qd->kd", weights_bf, grad_rows, preferred_element_type=jnp.float32)
    return (grad_query, grad_key, grad_value)


def join_pieces(own_piece, peer_piece, upper):
    return jnp.where(
        upper,
        jnp.concatenate([peer_piece, own_piece], axis=1),
        jnp.concatenate([own_piece, peer_piece], axis=1),
    )


def doubling(pieces, stride):
    position = lax.axis_index("seq")
    for level_bit in range(stride.bit_length() - 1):
        others = jax.tree.map(
            lambda part, own: part.astype(own.dtype),
            partner(as_sent(pieces), "seq", level_bit),
            pieces,
        )
        upper = position // 2**level_bit % 2 == 1
        pieces = tuple(
            (
                join_pieces(own_piece, peer_piece, upper)
                for own_piece, peer_piece in zip(pieces, others)
            )
        )
    return pieces


def halving(pieces, stride):
    position = lax.axis_index("seq")
    for level_bit in reversed(range(stride.bit_length() - 1)):
        upper = position // 2**level_bit % 2 == 1
        middle = pieces[0].shape[1] // 2
        staying = tuple(
            (jnp.where(upper, member[:, middle:], member[:, :middle]) for member in pieces)
        )
        outgoing = tuple(
            (jnp.where(upper, member[:, :middle], member[:, middle:]) for member in pieces)
        )
        arrived = jax.tree.map(
            lambda part, own: part.astype(own.dtype),
            partner(as_sent(outgoing), "seq", level_bit),
            outgoing,
        )
        pieces = tuple((own_part + peer_part for own_part, peer_part in zip(staying, arrived)))
    return pieces


def gather_group(pieces, stride):
    if stride == lax.axis_size("seq"):
        return (lax.all_gather(pieces[0], "seq", axis=1, tiled=True),)
    return doubling(pieces, stride)


def scatter_group(pieces, stride):
    if stride == lax.axis_size("seq"):
        return (lax.psum_scatter(pieces[0], "seq", scatter_dimension=1, tiled=True),)
    return halving(pieces, stride)


def per_device(queries, keys, values, offsets, w_out, grad_mixed):
    row_count, local_width = queries.shape
    head_count = local_width // HD
    first_head = lax.axis_index("head") * head_count
    seq_count = lax.axis_size("seq")
    chosen = lax.dynamic_slice_in_dim(offsets, first_head, head_count, 1)
    query_cube = queries.reshape(row_count, head_count, HD)
    key_cube = keys.reshape(row_count, head_count, HD)
    value_cube = values.reshape(row_count, head_count, HD)
    levels = [(1, jnp.zeros((head_count,), jnp.int32)), (G_MID, chosen[0]), (seq_count, chosen[1])]
    stored = []
    placed = []
    for stride, offset in levels:
        own_query = pick_rows(query_cube, stride, offset)
        own_key = pick_rows(key_cube, stride, offset)
        own_value = pick_rows(value_cube, stride, offset)
        key_value = gather_group((jnp.stack([own_key, own_value]),), stride)[0]
        stored.append((own_query, own_key, own_value, key_value[0], key_value[1]))
        lse_sel = lax.map(head_lse, (to_heads(own_query), to_heads(key_value[0]))).T
        marked = put_rows(jnp.ones_like(lse_sel), stride, offset) > 0.5
        placed.append((put_rows(lse_sel, stride, offset), marked))
    first_lse = placed[0][0]
    highest = first_lse
    for level_lse, marked in placed[1:]:
        highest = jnp.maximum(highest, jnp.where(marked, level_lse, highest))
    summed = jnp.exp(first_lse - highest)
    for level_lse, marked in placed[1:]:
        summed = summed + jnp.where(
            marked, jnp.exp(jnp.where(marked, level_lse, highest) - highest), 0.0
        )
    lse_all = highest + jnp.log(summed)
    attended = jnp.zeros((row_count, head_count, HD), jnp.float32)
    for (stride, offset), (own_query, own_key, own_value, key_all, value_all) in zip(
        levels, stored
    ):
        own_lse = pick_rows(lse_all, stride, offset)
        level_out = lax.map(
            head_out, (to_heads(own_query), to_heads(key_all), to_heads(value_all), own_lse.T)
        )
        attended = attended + put_rows(from_heads(level_out), stride, offset)
    attended = attended.astype(jnp.bfloat16)
    flat_attended = attended.reshape(row_count, local_width)
    partial_value = jnp.dot(flat_attended, w_out, preferred_element_type=jnp.float32)
    mixed = lax.psum_scatter(partial_value, "head", scatter_dimension=1, tiled=True).astype(
        jnp.bfloat16
    )
    grad_full = lax.all_gather(grad_mixed, "head", axis=1, tiled=True)
    grad_flat = lax.dot_general(
        grad_full, w_out, (((1,), (1,)), ((), ())), preferred_element_type=jnp.float32
    ).astype(jnp.bfloat16)
    weight_part = lax.dot_general(
        flat_attended, grad_full, (((0,), (0,)), ((), ())), preferred_element_type=jnp.float32
    )
    grad_w_out = lax.psum(weight_part, "seq")
    grad_cube = grad_flat.reshape(row_count, head_count, HD)
    delta_all = jnp.sum(grad_cube.astype(jnp.float32) * attended.astype(jnp.float32), axis=2)
    grad_q_sum = jnp.zeros((row_count, head_count, HD), jnp.float32)
    grad_k_sum = jnp.zeros((row_count, head_count, HD), jnp.float32)
    grad_v_sum = jnp.zeros((row_count, head_count, HD), jnp.float32)
    for (stride, offset), (own_query, own_key, own_value, key_all, value_all) in zip(
        levels, stored
    ):
        own_grad = pick_rows(grad_cube, stride, offset)
        own_lse = pick_rows(lse_all, stride, offset)
        own_delta = pick_rows(delta_all, stride, offset)
        if stride == 1:
            grad_query, grad_key, grad_value = lax.map(
                head_grads,
                (
                    to_heads(own_query),
                    to_heads(key_all),
                    to_heads(value_all),
                    to_heads(own_grad),
                    own_lse.T,
                    own_delta.T,
                ),
            )
            grad_key = from_heads(grad_key)
            grad_value = from_heads(grad_value)
        else:
            grad_query, key_all_grad, value_all_grad = lax.map(
                head_grads,
                (
                    to_heads(own_query),
                    to_heads(key_all),
                    to_heads(value_all),
                    to_heads(own_grad),
                    own_lse.T,
                    own_delta.T,
                ),
            )
            returned = scatter_group(
                (jnp.stack([from_heads(key_all_grad), from_heads(value_all_grad)]),), stride
            )[0]
            grad_key = returned[0]
            grad_value = returned[1]
        grad_q_sum = grad_q_sum + put_rows(from_heads(grad_query), stride, offset)
        grad_k_sum = grad_k_sum + put_rows(grad_key, stride, offset)
        grad_v_sum = grad_v_sum + put_rows(grad_value, stride, offset)
    grad_queries = grad_q_sum.astype(jnp.bfloat16).reshape(row_count, local_width)
    grad_keys = grad_k_sum.astype(jnp.bfloat16).reshape(row_count, local_width)
    grad_values = grad_v_sum.astype(jnp.bfloat16).reshape(row_count, local_width)
    return (mixed, grad_queries, grad_keys, grad_values, grad_w_out)


def solution(mesh):
    in_specs = (
        P("seq", "head"),
        P("seq", "head"),
        P("seq", "head"),
        P(),
        P("head", None),
        P("seq", "head"),
    )
    out_specs = (
        P("seq", "head"),
        P("seq", "head"),
        P("seq", "head"),
        P("seq", "head"),
        P("head", None),
    )
    return jax.shard_map(
        per_device, mesh=mesh, in_specs=in_specs, out_specs=out_specs, check_vma=False
    )
```

profile of v0, /device:TPU:1, one launch (start us, length us, event | category | flops | bytes accessed | tf_op | source)
XLA Modules:
  0.0 895.3 jit_solution(8473471631777287982)
XLA Ops:
  8.1 14.3 %all_gather.7 = bf16[512,768]{1,0:T(8,128)(2,1)S(1)} all-gather(bf16[512,384]{1,0:T(8,128)(2,1)} %param.29), channel_id=1, replica_groups=mesh['seq'=64,'head'=2] {'head'}, dimensions={1}, use_global_device_ids=true | all-gather | bytes 1179648 | tf_op jit(solution)/shard_map/all_gather | solution.py:185
  25.3 1.6 reshape_reshape.40
  26.9 2.4 reshape_reshape.39
  30.8 4.4 select_reduce_fusion
  44.8 3.6 while.102
  50.5 4.2 select_reduce_fusion.4
  55.0 86.3 %all_gather.6 = bf16[2,512,6,64]{3,0,2,1:T(2,128)(2,1)S(1)} all-gather(bf16[2,8,6,64]{3,0,2,1:T(2,128)(2,1)S(1)} %copy.320), channel_id=1, replica_groups=mesh['seq'=64,'head'=2] {'seq'}, dimensions={1}, use_global_device_ids=true | all-gather | bytes 798720 | tf_op jit(solution)/shard_map/all_gather | solution.py:129
  141.3 2.2 fusion.214
  144.5 1.9 maximum_select_fusion.1
  146.4 3.1 while.104
  164.7 13.5 %while.103 = (s32[]{:T(128)}, f32[6,128]{1,0:T(8,128)}, bf16[6,128,64]{2,1,0:T(8,128)(2,1)S(1)}, bf16[6,512,64]{2,1,0:T(8,128)(2,1)S(1)}, s32[]{:T(128)}, /*index=5*/s32[]{:T(128)}) while((s32[]{:T(128)}, f32[6,128]{1,0:T(8,128)}, bf16[6,128,64]{2,1,0:T(8,128)(2,1)S(1)}, bf16[6,512,64]{2,1,0:T(8,128)(2,1)S(1)}, s32[]{:T(128)}, ...), condition=%wide.region_10.11_spmd, body=%wide.region_7.10_spmd.sunk | while | flops 8650626 | bytes 693329 | solution.py:157
  178.3 3.1 broadcast_select_fusion
  181.4 1.8 select_n.370
  185.3 16.3 %while.107 = (s32[]{:T(128)}, f32[6,8,64]{2,1,0:T(8,128)}, bf16[6,8,64]{2,1,0:T(8,128)(2,1)S(1)}, bf16[6,512,64]{2,1,0:T(8,128)(2,1)S(1)}, f32[6,8]{1,0:T(8,128)}, /*index=5*/bf16[6,512,64]{2,1,0:T(8,128)(2,1)S(1)}, s32[]{:T(128)}) while((s32[]{:T(128)}, f32[6,8,64]{2,1,0:T(8,128)}, bf16[6,8,64]{2,1,0:T(8,128)(2,1)S(1)}, ...), condition=%wide.region_25.26_spmd, body=%wide.region_24.25_spmd.sunk | while | flops 1060866 | bytes 271001 | solution.py:175
  208.0 2.2 copy.331
  210.8 15.7 %while.106 = (s32[]{:T(128)}, f32[6,128,64]{1,2,0:T(8,128)}, bf16[6,128,64]{2,1,0:T(8,128)(2,1)S(1)}, bf16[6,512,64]{2,1,0:T(8,128)(2,1)}, f32[6,128]{1,0:T(8,128)}, /*index=5*/bf16[6,512,64]{2,1,0:T(8,128)(2,1)}, s32[]{:T(128)}) while((s32[]{:T(128)}, f32[6,128,64]{1,2,0:T(8,128)}, bf16[6,128,64]{2,1,0:T(8,128)(2,1)S(1)}, ...), condition=%wide.region_22.23_spmd, body=%wide.region_21.22_spmd.sunk | while | flops 16973824 | bytes 331353 | solution.py:175
  211.5 1.9 fusion.304
  214.1 1.9 fusion.304
  216.8 1.9 fusion.304
  219.4 1.9 fusion.304
  222.0 1.9 fusion.304
  224.6 1.9 fusion.304
  226.6 2.0 copy.374
  228.6 1.8 copy.332
  232.0 1.8 broadcast_in_dim.469
  236.2 20.4 %while.105 = (s32[]{:T(128)}, f32[6,512,64]{1,2,0:T(8,128)}, bf16[6,512,64]{2,1,0:T(8,128)(2,1)S(1)}, bf16[6,512,64]{2,1,0:T(8,128)(2,1)S(1)}, f32[6,512]{1,0:T(8,128)}, /*index=5*/bf16[6,512,64]{2,1,0:T(8,128)(2,1)}, s32[]{:T(128)}) while((s32[]{:T(128)}, f32[6,512,64]{1,2,0:T(8,128)}, bf16[6,512,64]{2,1,0:T(8,128)(2,1)S(1)}, ...), condition=%wide.region_19.20_spmd, body=%wide.region_18.19_spmd.sunk | while | flops 67895296 | bytes 532569 | solution.py:175
  237.5 2.1 fusion.299
  240.9 2.1 fusion.299
  244.3 2.1 fusion.299
  247.7 2.1 fusion.299
  251.1 2.1 fusion.299
  254.6 2.1 fusion.299
  256.7 2.4 broadcast_in_dim.488
  259.1 2.7 copy.340
  261.8 2.5 multiply_reduce_fusion
  264.4 1.9 reshape.406
  267.6 2.5 broadcast_in_dim.488.clone
  270.1 2.6 broadcast_in_dim.489
  272.8 2.3 copy.334
  275.0 1.8 select_reduce_fusion.8
  280.9 30.3 %while.110 = (s32[]{:T(128)}, f32[6,8,64]{2,1,0:T(8,128)}, f32[6,512,64]{1,2,0:T(8,128)}, f32[6,512,64]{1,2,0:T(8,128)}, bf16[6,8,64]{2,1,0:T(8,128)(2,1)S(1)}, ...) while((s32[]{:T(128)}, f32[6,8,64]{2,1,0:T(8,128)}, ...), condition=%wide.region_37.38_spmd, body=%wide.region_36.37_spmd.sunk | while | flops 2650114 | bytes 747289 | solution.py:219
  311.1 2.6 pad_maximum_fusion
  313.8 5.4 copy.359
  319.2 1.7 fusion.164
  325.2 39.0 %while.109 = (s32[]{:T(128)}, f32[6,128,64]{1,2,0:T(8,128)}, f32[6,512,64]{1,2,0:T(8,128)S(1)}, f32[6,512,64]{1,2,0:T(8,128)}, bf16[6,128,64]{2,1,0:T(8,128)(2,1...) while((s32[]{:T(128)}, f32[6,128,64]{1,2,0:T(8,128)}, ...), condition=%wide.region_33.34_spmd, body=%wide.region_32.33_spmd.sunk | while | flops 42401792 | bytes 2007161 | solution.py:219
  328.1 1.7 fusion.338
  330.1 1.6 fusion.340
  334.6 1.7 fusion.338
  341.1 1.7 fusion.338
  343.1 1.6 fusion.340
  347.6 1.7 fusion.338
  354.1 1.7 fusion.338
  356.1 1.6 fusion.340
  360.6 1.7 fusion.338
  364.2 2.0 select_convert_fusion
  368.9 2.7 fusion.215
  371.6 6.1 collective-permute-done.2
  383.8 26.3 %while.108 = (s32[]{:T(128)}, f32[6,512,64]{1,2,0:T(8,128)S(1)}, f32[6,512,64]{1,2,0:T(8,128)}, f32[6,512,64]{1,2,0:T(8,128)}, bf16[6,512,64]{2,1,0:T(8,128)(2,1...) while((s32[]{:T(128)}, f32[6,512,64]{1,2,0:T(8,128)S(1)}, ...), condition=%wide.region_29.30_spmd, body=%wide.region_28.29_spmd.sunk | while | flops 169607168 | bytes 5915769 | solution.py:205
  417.2 2.4 copy.351
  423.3 2.3 copy.363
  429.2 2.3 copy.358
  431.5 442.2 %all-reduce.4.cloned.1.call-done = (f32[2,512,6,64]{3,0,2,1:T(2,128)}, f32[384,768]{1,0:T(8,128)}) async-done(((f32[2,512,6,64]{3,0,2,1:T(2,128)}, f32[384,768]{1,0:T(8,128)}), (f32[2,512,6,64]{3,0,2,1:T(2,128)}, f32[384,768]{1,0:T(8,128)})) %all-reduce.4.cloned.1.call-update) | async-done | bytes 2752528
  878.4 3.7 fusion.173
  884.9 1.9 convert_element_type.106
  (380 shorter events, 214.1 us)
Async XLA Ops:
  8.0 15.3 %copy-start = (bf16[384,768]{1,0:T(8,128)(2,1)S(1)}, bf16[384,768]{1,0:T(8,128)(2,1)}, u32[]{:S(2)}) copy-start(bf16[384,768]{1,0:T(8,128)(2,1)} %param.28) | copy-start | bytes 1769476
  8.0 865.7 %all-reduce.4.cloned.1.call-start = ((), (), s32[]{:S(2)}) async-start(), calls=%async_computation.2 | async-start | bytes 8650752
  22.4 0.9 copy-start.15
  23.8 0.8 copy-start.34
  24.6 4.7 copy-start.17
  35.3 4.5 copy-start.18
  36.4 3.1 copy-start.22
  37.6 1.9 copy-start.24
  37.6 3.6 copy-start.19
  38.3 105.6 %collective-permute-start = (bf16[2,128,6,64]{1,3,2,0:T(8,128)(2,1)}, bf16[2,128,6,64]{1,3,2,0:T(8,128)(2,1)}, u32[]{:S(2)}, u32[]{:S(2)}) collective-permute-start(bf16[2,128,6,64]{1,3,2,0:T(8,128)(2,1)} %pad_maximum_fusion.2), channel_id=1, source_target_pairs={{0,2},{2,0},{4,6},{6,4},{8,10},{10,8},{12,14},{14,12},{16,18},{18,... | collective-permute-start | bytes 589832 | tf_op jit(solution)/shard_map/ppermute | solution.py:17
  41.4 7.8 copy-start.11
  48.4 6.3 copy-start.1
  48.4 6.3 copy-start.3
  48.4 102.4 %copy-start.28 = (f32[6,512]{1,0:T(8,128)}, f32[6,512]{1,0:T(8,128)S(1)}, u32[]{:S(2)}) copy-start(f32[6,512]{1,0:T(8,128)S(1)} %get-tuple-element.329) | copy-start | bytes 36868
  49.2 102.3 %copy-start.31 = (pred[64,6]{0,1:T(8,128)(4,1)}, pred[64,6]{0,1:T(8,128)(4,1)S(1)}, u32[]{:S(2)}) copy-start(pred[64,6]{0,1:T(8,128)(4,1)S(1)} %get-tuple-element.852) | copy-start | bytes 1156
  143.5 0.9 copy-start.23
  143.5 0.9 copy-start.25
  143.9 11.0 %copy-start.36 = (pred[4,6]{1,0:T(4,128)(4,1)S(1)}, pred[4,6]{1,0:T(4,128)(4,1)}, u32[]{:S(2)}) copy-start(pred[4,6]{1,0:T(4,128)(4,1)} %get-tuple-element.853) | copy-start | bytes 76
  143.9 14.3 %copy-start.12 = (bf16[512,384]{0,1:T(8,128)(2,1)S(1)}, bf16[512,384]{0,1:T(8,128)(2,1)}, u32[]{:S(2)}) copy-start(bf16[512,384]{0,1:T(8,128)(2,1)} %copy-done.11) | copy-start | bytes 1179652
  146.4 14.4 %collective-permute-start.1 = (bf16[2,256,6,64]{1,3,2,0:T(8,128)(2,1)}, bf16[2,256,6,64]{1,3,2,0:T(8,128)(2,1)}, u32[]{:S(2)}, u32[]{:S(2)}) collective-permute-start(bf16[2,256,6,64]{1,3,2,0:T(8,128)(2,1)} %maximum_select_fusion.1), channel_id=1, source_target_pairs={{0,4},{2,6},{4,0},{6,2},{8,12},{10,14},{12,8},{14,10},{16,20},{18,... | collective-permute-start | bytes 1179656 | tf_op jit(solution)/shard_map/ppermute | solution.py:17
  149.5 3.0 copy-start.30
  149.5 9.9 %copy-start.21 = (bf16[128,6,64]{2,1,0:T(8,128)(2,1)S(1)}, bf16[128,6,64]{2,1,0:T(8,128)(2,1)}, u32[]{:S(2)}) copy-start(bf16[128,6,64]{2,1,0:T(8,128)(2,1)} %get-tuple-element.698) | copy-start | bytes 294916
  149.7 10.4 %copy-start.32 = (pred[4,6]{0,1:T(8,128)(4,1)}, pred[4,6]{0,1:T(8,128)(4,1)S(1)}, u32[]{:S(2)}) copy-start(pred[4,6]{0,1:T(8,128)(4,1)S(1)} %copy.312) | copy-start | bytes 76
  155.0 5.8 copy-start.33
  158.2 1.9 copy-start.27
  178.3 23.4 %copy-start.5 = (bf16[6,512,64]{2,1,0:T(8,128)(2,1)}, bf16[6,512,64]{2,1,0:T(8,128)(2,1)S(1)}, u32[]{:S(2)}) copy-start(bf16[6,512,64]{2,1,0:T(8,128)(2,1)S(1)} %get-tuple-element.1484) | copy-start | bytes 1179652
  201.6 0.9 copy-start.7
  226.6 9.7 %copy-start.2 = (bf16[6,512,64]{2,1,0:T(8,128)(2,1)S(1)}, bf16[6,512,64]{2,1,0:T(8,128)(2,1)}, u32[]{:S(2)}) copy-start(bf16[6,512,64]{2,1,0:T(8,128)(2,1)} %copy-done.1) | copy-start | bytes 1179652
  226.6 9.7 %copy-start.4 = (bf16[6,512,64]{2,1,0:T(8,128)(2,1)S(1)}, bf16[6,512,64]{2,1,0:T(8,128)(2,1)}, u32[]{:S(2)}) copy-start(bf16[6,512,64]{2,1,0:T(8,128)(2,1)} %copy-done.3) | copy-start | bytes 1179652
  313.8 5.4 copy-start.6
  313.8 5.4 copy-start.29
  319.2 2.4 copy-start.16
  320.9 0.7 copy-start.10
  323.1 561.8 %reduce-scatter.2.cloned.1.call-start = ((), (), s32[]{:S(2)}) async-start(), calls=%async_computation.1 | async-start | bytes 2359296 | tf_op jit(solution)/shard_map/reduce_scatter | solution.py:182
  364.2 3.4 copy-start.35
  366.2 11.5 %collective-permute-start.2 = (bf16[2,256,6,64]{1,3,2,0:T(8,128)(2,1)}, bf16[2,256,6,64]{1,3,2,0:T(8,128)(2,1)}, u32[]{:S(2)}, u32[]{:S(2)}) collective-permute-start(bf16[2,256,6,64]{1,3,2,0:T(8,128)(2,1)} %select_convert_fusion), channel_id=1, source_target_pairs={{0,4},{2,6},{4,0},{6,2},{8,12},{10,14},{12,8},{14,10},{16,20},{18,... | collective-permute-start | bytes 1179656 | tf_op jit(solution)/shard_map/ppermute | solution.py:17
  379.1 0.9 copy-start.8
  380.7 38.9 %collective-permute-start.3 = (bf16[2,128,6,64]{1,3,2,0:T(8,128)(2,1)}, bf16[2,128,6,64]{1,3,2,0:T(8,128)(2,1)S(1)}, u32[]{:S(2)}, u32[]{:S(2)}) collective-permute-start(bf16[2,128,6,64]{1,3,2,0:T(8,128)(2,1)} %select_convert_fusion.1), channel_id=1, source_target_pairs={{0,2},{2,0},{4,6},{6,4},{8,10},{10,8},{12,14},{14,12},{16,18},{18,... | collective-permute-start | bytes 589832 | tf_op jit(solution)/shard_map/ppermute | solution.py:17
  410.2 0.9 copy-start.14
  412.4 1.3 copy-start.26
  417.2 2.4 copy-start.9
  877.1 1.3 copy-start.13
  883.1 3.8 copy-start.20
Sparse Core Ops, SparseCore 0:
  323.3 550.4 all-reduce.3
Sparse Core Ops, SparseCore 1:
  371.7 29.0 reduce-scatter.1
where the time goes:
time: 901 us; the launch traced here: 895 us
  waiting for transfers between devices  448 us (50%)
  local copies, waits for them, and re-layouts  152 us (17%)
  matrix products  126 us (14%)
  blocking collectives  101 us (11%)
  other arithmetic  46.9 us (5%)
  between operations  16.7 us (2%)
    unnamed x3, waiting for transfers between devices  442 us
    all_gather x1, blocking collectives, gather_group(): return (lax.all_gather(pieces[0], 'seq', axis=1, tiled=True),)  86.3 us
    broadcast_in_dim x40, local copies, waits for them, and re-layouts, put_rows(): spread = jnp.where(hits, source[:, None], jnp.zeros((), source.dtype))  46.9 us
    dot_general x18, matrix products, head_out(): jnp.einsum('qk,kd->qd', weights_bf, value_rows, preferred_element_type=jn...  33.4 us
    dot_general x18, matrix products, head_grads(): jnp.einsum('qk,qd->kd', weights_bf, grad_rows, preferred_element_type=jnp...  24 us
    dot_general x18, matrix products, score_grads(): jnp.einsum('qd,kd->qk', grad_rows, value_rows, preferred_element_type=jnp...  20.6 us
  transfers between devices with their start and end apart: 6, of which 2 were waited for; matrix products, arithmetic and copies ran while one was open for 16% of the time, Pallas kernels for 0%

commit v1 on v0

v1 whole, which is shorter than its diff:
```python
import math

import jax
import jax.numpy as jnp
from jax import lax
from jax.experimental import pallas as pl
from jax.experimental.pallas import tpu as pltpu
from jax.sharding import PartitionSpec as P

HD = 64
TOK = 512
CHIPS = 32
OWNERS = 24
SCALE = 0.125 * math.log2(math.e)
MESH = pl.DeviceIdType.MESH
F32 = jnp.float32
BF16 = jnp.bfloat16


def nn(a, b):
    return lax.dot_general(a, b, (((1,), (0,)), ((), ())), preferred_element_type=F32)


def nt(a, b):
    return lax.dot_general(a, b, (((1,), (1,)), ((), ())), preferred_element_type=F32)


def tn(a, b):
    return lax.dot_general(a, b, (((0,), (0,)), ((), ())), preferred_element_type=F32)


def iota(shape, dim):
    return lax.broadcasted_iota(jnp.int32, shape, dim)


def halves(x):
    hi = x.astype(BF16)
    return hi, (x - hi.astype(F32)).astype(BF16)


def thirds(x):
    hi = x.astype(BF16).astype(F32)
    mid = (x - hi).astype(BF16).astype(F32)
    return [hi, mid, x - hi - mid]


def cols(p):
    return pl.ds(pl.multiple_of(p * 128, 128), 128)


def kernel(
    off_ref, q_ref, k_ref, v_ref, w_ref, g_ref,
    mixed_ref, dq_ref, dk_ref, dv_ref, dw_ref,
    kv1, x2, goth, qt, kt, vt, k1t, q1t, q2, e1, e2, p0, p1, p2, o0, o1, o2, st0, st1, st2,
    at, an, gs, gt, mxs, mxr, wps, wpo, wmr, wrs, wrr, wfull,
    do2, de2, dx, dxs, dxm, dxb, xr, dq2, dqx, dk1, dks, dkm, dkc, dkr, dk0, dv0,
    ssem, rsem,
):
    s = lax.axis_index("seq")
    h = lax.axis_index("head")
    chip, core = s // 2, lax.rem(s, 2)
    r = lax.rem(s, 4)
    mate = s + 1 - 2 * core
    side = lax.rem(chip, 2)
    facing = s + 2 - 4 * side
    r_mate = r + 1 - 2 * core
    r_facing = r + 2 - 4 * side
    r_other = r_mate + 2 - 4 * side
    first = h * 6
    to_mate, to_facing, to_half = (mate, h), (facing, h), (s, 1 - h)

    def peer(c):
        return (2 * c + core, h)

    def copy(src, dst, n, device):
        return pltpu.make_async_remote_copy(
            src_ref=src, dst_ref=dst, send_sem=ssem.at[n], recv_sem=rsem.at[n],
            device_id=device, device_id_type=MESH,
        )

    barrier = pltpu.get_barrier_semaphore()

    def greet(i, carry):
        pl.semaphore_signal(
            barrier, inc=1, device_id=peer(lax.rem(chip + i, CHIPS)), device_id_type=MESH
        )
        return carry

    lax.fori_loop(1, CHIPS, greet, 0)
    for device in (to_mate, to_half):
        pl.semaphore_signal(barrier, inc=1, device_id=device, device_id_type=MESH)
    pl.semaphore_wait(barrier, CHIPS + 1)

    send_g = copy(g_ref, goth, 0, to_half)
    send_g.start()

    lane128 = iota((1, 128), 1)
    lane256 = iota((1, 256), 1)
    lane512 = iota((1, TOK), 1)
    row128 = iota((128, 1), 0)
    row16 = iota((16, 1), 0)
    pair16 = (row16 < 8) == (lane128 < HD)

    q2[...] = jnp.zeros_like(q2)
    do2[...] = jnp.zeros_like(do2)

    def pick(p, carry):
        q, k, v = q_ref[:, cols(p)], k_ref[:, cols(p)], v_ref[:, cols(p)]
        kv = jnp.concatenate([k, v], axis=1)
        rows, columns = iota((128, TOK), 0), iota((128, TOK), 1)
        hits = []
        for j in range(2):
            f1 = off_ref[0, first + 2 * p + j]
            hit = jnp.where(columns == rows * 4 + f1, 1.0, 0.0).astype(BF16)
            e1[2 * p + j] = hit
            hits.append(hit)
        f2 = jnp.where(row16 < 8, off_ref[1, first + 2 * p], off_ref[1, first + 2 * p + 1])
        hit2 = jnp.where(
            iota((16, TOK), 1) == lax.rem(iota((16, TOK), 0), 8) * 64 + f2, 1.0, 0.0
        ).astype(BF16)
        e2[p] = hit2
        left = lax.rem(lane256, 128) < HD
        picked = jnp.where(left, nn(hits[0], kv), nn(hits[1], kv)).astype(BF16)
        kv1[r, p, 0:128, :] = picked[:, 0:128]
        kv1[r, p, 128:256, :] = picked[:, 128:256]
        both = nn(hit2, kv)
        few = jnp.where(left, both[0:8], both[8:16])
        x2[core, chip, :, cols(p)] = jnp.concatenate([few[:, 0:128], few[:, 128:256]], axis=0).astype(BF16)
        q2[pl.ds(pl.multiple_of(p * 16, 16), 16), cols(p)] = jnp.where(pair16, nn(hit2, q), 0.0).astype(BF16)
        q_t = q.T
        qt[p] = q_t
        kt[p] = k.T
        vt[p] = v.T
        for j in range(2):
            mine = (row128 < HD) if j == 0 else (row128 >= HD)
            q1t[2 * p + j] = jnp.where(mine, nt(q_t, hits[j]), 0.0).astype(BF16)
        return carry

    lax.fori_loop(0, 3, pick, 0)

    send_a = copy(kv1.at[r], kv1.at[r], 2, to_facing)
    send_a.start()
    send_b = copy(kv1.at[r], kv1.at[r], 1, to_mate)
    send_b.start()

    def spread(i, carry):
        copy(x2.at[core, chip], x2.at[core, chip], 4, peer(lax.rem(chip + i, CHIPS))).start()
        return carry

    lax.fori_loop(1, CHIPS, spread, 0)

    def forward(keys, q_masked, v_t, width):
        scores = nn(keys, q_masked)
        top = jnp.max(scores, axis=0, keepdims=True)
        weights = jnp.exp2((scores - top) * SCALE).astype(BF16)
        out = nn(jnp.concatenate([v_t, jnp.ones((16, TOK), BF16)], axis=0), weights)
        return weights, out, top

    def masked(x_t, j):
        mine = (row128 < HD) if j == 0 else (row128 >= HD)
        return jnp.where(mine, x_t, jnp.zeros((), x_t.dtype))

    def near(p, carry):
        k, q_t, v_t = k_ref[:, cols(p)], qt[p], vt[p]
        for j in range(2):
            weights, out, top = forward(k, masked(q_t, j), v_t[HD * j : HD * (j + 1)], TOK)
            p0[2 * p + j] = weights
            o0[2 * p + j] = out[0:HD]
            st0[2 * p + j, 0:1] = top
            st0[2 * p + j, 1:2] = out[HD : HD + 1]
        return carry

    lax.fori_loop(0, 2, near, 0)
    arrived_a = copy(kv1.at[r_facing], kv1.at[r_facing], 2, to_facing)
    arrived_a.wait_recv()
    send_c = copy(kv1.at[r_facing], kv1.at[r_facing], 3, to_mate)
    send_c.start()
    lax.fori_loop(2, 3, near, 0)
    copy(x2.at[core, pl.ds(0, 31)], x2.at[core, pl.ds(0, 31)], 4, to_mate).wait_recv()
    send_d = copy(x2.at[core], x2.at[core], 5, to_mate)
    send_d.start()

    copy(kv1.at[r_mate], kv1.at[r_mate], 1, to_mate).wait_recv()
    copy(kv1.at[r_other], kv1.at[r_other], 3, to_mate).wait_recv()

    def middle(p, carry):
        keys = kv1[:, p, 0:128, :].reshape(TOK, 128)
        values = kv1[:, p, 128:256, :].reshape(TOK, 128)
        k1t[p] = keys.T
        v_t = values.T
        for j in range(2):
            weights, out, top = forward(keys, q1t[2 * p + j], v_t[HD * j : HD * (j + 1)], 128)
            p1[2 * p + j] = weights
            hi, lo = halves(out[0:HD])
            stats = jnp.concatenate(
                thirds(out[HD : HD + 1]) + thirds(top) + [jnp.zeros((10, 128), F32)], axis=0
            ).astype(BF16)
            wide = nn(jnp.concatenate([hi, lo, stats], axis=0), e1[2 * p + j])
            o1[2 * p + j] = wide[0:HD] + wide[HD : 2 * HD]
            st1[2 * p + j, 1:2] = jnp.sum(wide[128:131], axis=0, keepdims=True)
            st1[2 * p + j, 0:1] = jnp.sum(wide[131:134], axis=0, keepdims=True)
        return carry

    lax.fori_loop(0, 3, middle, 0)

    copy(x2.at[1 - core], x2.at[1 - core], 5, to_mate).wait_recv()
    own_head = iota((48, 384), 0) // 8 == iota((48, 384), 1) // HD
    xs = x2[...].reshape(1024, 384)
    scores = nt(q2[...], xs)
    scores = jnp.where(lax.rem(iota((1, 1024), 1), 16) < 8, scores, -1e30)
    top = jnp.max(scores, axis=1, keepdims=True)
    weights = jnp.exp2((scores - top) * SCALE).astype(BF16).astype(F32)
    p2[...] = weights
    o2[...] = jnp.where(own_head, nn(pltpu.roll(weights, 8, 1).astype(BF16), xs), 0.0)
    st2[0] = jnp.broadcast_to(top, (48, 128))
    st2[1] = jnp.broadcast_to(jnp.sum(weights, axis=1, keepdims=True), (48, 128))

    def expand2(part, hit2):
        hi, lo = halves(part)
        return tn(jnp.concatenate([hi, lo], axis=0), jnp.concatenate([hit2, hit2], axis=0))

    def merge(p, carry):
        hit2 = e2[p]
        hit2_wide = hit2.astype(F32)
        sixteen = pl.ds(pl.multiple_of(p * 16, 16), 16)
        far = expand2(o2[sixteen, cols(p)], hit2)
        top2 = hit2_wide * st2[0, sixteen, 0:1]
        sum2 = hit2_wide * st2[1, sixteen, 0:1]
        found = []
        for j in range(2):
            n = 2 * p + j
            eight = slice(8 * j, 8 * j + 8)
            chosen1 = lax.rem(lane512, 4) == off_ref[0, first + n]
            chosen2 = lax.rem(lane512, 64) == off_ref[1, first + n]
            m0, l0 = st0[n, 0:1], st0[n, 1:2]
            m1, l1 = jnp.where(chosen1, st1[n, 0:1], -1e30), st1[n, 1:2]
            m2 = jnp.where(chosen2, jnp.sum(top2[eight], axis=0, keepdims=True), -1e30)
            l2 = jnp.sum(sum2[eight], axis=0, keepdims=True)
            highest = jnp.maximum(m0, jnp.maximum(m1, m2))
            c0 = jnp.exp2((m0 - highest) * SCALE)
            c1 = jnp.exp2((m1 - highest) * SCALE)
            c2 = jnp.exp2((m2 - highest) * SCALE)
            over = 1.0 / (c0 * l0 + c1 * l1 + c2 * l2)
            g0, g1, g2 = c0 * over, c1 * over, c2 * over
            gs[n, 0:1] = g0
            gs[n, 1:2] = g1
            gs[n, 2:3] = g2
            found.append(g0 * o0[n] + g1 * o1[n] + g2 * far[HD * j : HD * (j + 1)])
        both = jnp.concatenate(found, axis=0)
        at[pl.ds(pl.multiple_of(p * 128, 128), 128), :] = both.astype(BF16)
        an[:, cols(p)] = both.T.astype(BF16)
        return carry

    lax.fori_loop(0, 3, merge, 0)

    own_cols = pl.ds(pl.multiple_of(h * 384, 128), 384)
    other_cols = pl.ds(pl.multiple_of((1 - h) * 384, 128), 384)
    mxs[...] = nn(an[...], w_ref[:, other_cols]).astype(BF16)
    send_m = copy(mxs, mxr, 6, to_half)
    send_m.start()

    copy(goth, goth, 0, to_half).wait_recv()

    mate_rows = pl.ds(pl.multiple_of((1 - core) * 192, 64), 192)
    own_rows = pl.ds(pl.multiple_of(core * 192, 64), 192)
    wps[pl.ds(h * 12, 12)] = nn(at[mate_rows, :], g_ref[...]).astype(BF16).reshape(12, 16, 384)
    wps[pl.ds((1 - h) * 12, 12)] = nn(at[mate_rows, :], goth[...]).astype(BF16).reshape(12, 16, 384)
    send_w = copy(wps, wmr, 7, to_mate)
    send_w.start()

    gt[...] = (nt(w_ref[:, own_cols], g_ref[...]) + nt(w_ref[:, other_cols], goth[...])).astype(BF16)

    def shares(p, carry):
        hit2 = e2[p]
        hit2_wide = hit2.astype(F32)
        sixteen = pl.ds(pl.multiple_of(p * 16, 16), 16)
        grads = []
        deltas = []
        for j in range(2):
            n = 2 * p + j
            own = pl.ds(pl.multiple_of(p * 128 + j * HD, HD), HD)
            grad = gt[own, :].astype(F32)
            delta = jnp.sum(grad * at[own, :].astype(F32), axis=0, keepdims=True)
            gs[n, 3:4] = delta
            weight = 0.125 * gs[n, 2:3]
            grads.append((grad * weight).astype(BF16))
            deltas.append(
                jnp.sum(hit2_wide[8 * j : 8 * j + 8] * (weight * delta), axis=1, keepdims=True)
            )
        few = nt(hit2, jnp.concatenate(grads, axis=0))
        do2[sixteen, cols(p)] = jnp.where(pair16, few, 0.0).astype(BF16)
        de2[sixteen, :] = jnp.broadcast_to(jnp.concatenate(deltas, axis=0), (16, 128))
        return carry

    lax.fori_loop(0, 3, shares, 0)

    xs = x2[...].reshape(1024, 384)
    weights = p2[...]
    grad_prob = pltpu.roll(nt(do2[...], xs), 1024 - 8, 1)
    dscore = weights * (grad_prob - de2[:, 0:1])
    dscore_b = dscore.astype(BF16)
    dq2[...] = jnp.where(own_head, nn(dscore_b, xs), 0.0)
    left_side = jnp.concatenate([dscore, 8.0 * pltpu.roll(weights, 8, 1)], axis=0).astype(BF16)
    dx[...] = tn(left_side, jnp.concatenate([q2[...], do2[...]], axis=0)).reshape(2, CHIPS, 16, 384)
    dxs[...] = dx[1 - core].astype(BF16)
    send_x = copy(dxs, dxm, 11, to_mate)
    send_x.start()

    wpo[pl.ds(h * 12, 12)] = nn(at[own_rows, :], g_ref[...]).reshape(12, 16, 384)
    wpo[pl.ds((1 - h) * 12, 12)] = nn(at[own_rows, :], goth[...]).reshape(12, 16, 384)
    copy(wmr, wmr, 7, to_mate).wait_recv()
    wrs[...] = (wpo[...] + wmr[...].astype(F32)).astype(BF16)
    owner = chip < OWNERS

    def reduce_w(i, carry):
        c = lax.rem(chip + i, OWNERS)

        @pl.when(c != chip)
        def _():
            copy(wrs.at[c], wrr.at[chip], 8, peer(c)).start()

        return carry

    lax.fori_loop(0, OWNERS, reduce_w, 0)

    def middle_back(p, carry):
        values = kv1[:, p, 128:256, :].reshape(TOK, 128)
        dscores, probs, q_all, g_all = [], [], [], []
        for j in range(2):
            n = 2 * p + j
            own = pl.ds(pl.multiple_of(p * 128 + j * HD, HD), HD)
            weight = 0.125 * gs[n, 1:2]
            grad = (gt[own, :].astype(F32) * weight).astype(BF16)
            stats = jnp.concatenate(
                thirds(weight * gs[n, 3:4]) + [jnp.zeros((13, TOK), F32)], axis=0
            ).astype(BF16)
            few = nt(jnp.concatenate([grad, stats], axis=0), e1[n])
            delta = jnp.sum(few[HD : HD + 3], axis=0, keepdims=True)
            nothing = jnp.zeros((HD, 128), BF16)
            part = few[0:HD].astype(BF16)
            grad_m = jnp.concatenate([part, nothing] if j == 0 else [nothing, part], axis=0)
            prob = p1[n]
            dscore = (prob.astype(F32) * (nn(values, grad_m) - delta)).astype(BF16)
            hi, lo = halves(nn(k1t[p, HD * j : HD * (j + 1), :], dscore))
            wide = nn(jnp.concatenate([hi, lo], axis=0), e1[n])
            dqx[n] = wide[0:HD] + wide[HD : 2 * HD]
            dscores.append(dscore)
            probs.append(prob)
            q_all.append(q1t[n])
            g_all.append(grad_m)
        grad_k = nt(jnp.concatenate(dscores, axis=1), jnp.concatenate(q_all, axis=1))
        grad_v = 8.0 * nt(jnp.concatenate(probs, axis=1), jnp.concatenate(g_all, axis=1))
        dk1[:, p, 0:128, :] = grad_k.reshape(4, 128, 128)
        dk1[:, p, 128:256, :] = grad_v.reshape(4, 128, 128)
        return carry

    lax.fori_loop(0, 3, middle_back, 0)
    dks[0] = dk1[r_mate].astype(BF16)
    dks[1] = dk1[r_other].astype(BF16)
    send_k = copy(dks, dkm, 13, to_mate)
    send_k.start()

    copy(dxm, dxm, 11, to_mate).wait_recv()
    dxb[...] = (dx[core] + dxm[...].astype(F32)).astype(BF16)

    def reduce_x(i, carry):
        c = lax.rem(chip + i, CHIPS)
        copy(dxb.at[c], xr.at[chip], 12, peer(c)).start()
        return carry

    lax.fori_loop(1, CHIPS, reduce_x, 0)

    copy(dkm, dkm, 13, to_mate).wait_recv()
    dkc[...] = (dk1[r_facing] + dkm[1].astype(F32)).astype(BF16)
    send_f = copy(dkc, dkr, 14, to_facing)
    send_f.start()

    def near_back(p, carry):
        k_t, q_t, v = kt[p], qt[p], v_ref[:, cols(p)]
        grad_k = jnp.zeros((TOK, 128), F32)
        grad_v = jnp.zeros((TOK, 128), F32)
        grad_q = []
        for j in range(2):
            n = 2 * p + j
            own = pl.ds(pl.multiple_of(p * 128 + j * HD, HD), HD)
            weight = 0.125 * gs[n, 0:1]
            grad = (gt[own, :].astype(F32) * weight).astype(BF16)
            nothing = jnp.zeros((HD, TOK), BF16)
            grad_m = jnp.concatenate([grad, nothing] if j == 0 else [nothing, grad], axis=0)
            prob = p0[n]
            dscore = (prob.astype(F32) * (nn(v, grad_m) - weight * gs[n, 3:4])).astype(BF16)
            grad_q.append(nn(k_t[HD * j : HD * (j + 1)], dscore) + dqx[n])
            grad_k = grad_k + nt(dscore, masked(q_t, j))
            grad_v = grad_v + nt(prob, grad_m)
        sixteen = pl.ds(pl.multiple_of(p * 16, 16), 16)
        total = jnp.concatenate(grad_q, axis=0) + expand2(dq2[sixteen, cols(p)], e2[p])
        dq_ref[:, cols(p)] = total.T.astype(BF16)
        dk0[p] = grad_k
        dv0[p] = 8.0 * grad_v
        return carry

    lax.fori_loop(0, 3, near_back, 0)

    @pl.when(owner)
    def _():
        wrr[chip] = wrs[chip]
        copy(wrr.at[pl.ds(0, 31)], wrr.at[pl.ds(0, 31)], 8, to_mate).wait_recv()
        wfull[core, chip] = jnp.sum(wrr[...].astype(F32), axis=0).astype(BF16)

        def give(i, carry):
            copy(wfull.at[core, chip], wfull.at[core, chip], 9, peer(lax.rem(chip + i, CHIPS))).start()
            return carry

        lax.fori_loop(1, CHIPS, give, 0)

    copy(mxr, mxr, 6, to_half).wait_recv()
    mixed_ref[...] = (nn(an[...], w_ref[:, own_cols]) + mxr[...].astype(F32)).astype(BF16)

    xr[chip] = dxb[chip]
    copy(xr.at[pl.ds(0, 31)], xr.at[pl.ds(0, 31)], 12, to_mate).wait_recv()
    far = jnp.sum(xr[...].astype(F32), axis=0)
    o2[0:16, :] = far
    copy(dkr, dkr, 14, to_facing).wait_recv()

    def finish(p, carry):
        left = lax.rem(lane256, 128) < HD
        near1 = dk1[r, p] + dkm[0, p].astype(F32) + dkr[p].astype(F32)
        near1 = jnp.concatenate([near1[0:128], near1[128:256]], axis=1)
        hit = jnp.concatenate([e1[2 * p], e1[2 * p + 1]], axis=0)
        near1 = jnp.concatenate([jnp.where(left, near1, 0.0), jnp.where(left, 0.0, near1)], axis=0)
        hi, lo = halves(near1)
        few = o2[0:16, cols(p)]
        few = jnp.concatenate([few[0:8], few[8:16]], axis=1)
        few = jnp.concatenate([jnp.where(left, few, 0.0), jnp.where(left, 0.0, few)], axis=0)
        total = tn(hit, hi) + tn(hit, lo) + expand2_right(few, e2[p])
        dk_ref[:, cols(p)] = (dk0[p] + total[:, 0:128]).astype(BF16)
        dv_ref[:, cols(p)] = (dv0[p] + total[:, 128:256]).astype(BF16)
        return carry

    def expand2_right(part, hit2):
        hi, lo = halves(part)
        return tn(jnp.concatenate([hit2, hit2], axis=0), jnp.concatenate([hi, lo], axis=0))

    lax.fori_loop(0, 3, finish, 0)

    def gathered(n_blocks):
        copy(wfull.at[core, pl.ds(0, n_blocks)], wfull.at[core, pl.ds(0, n_blocks)], 9, to_mate).wait_recv()
        copy(wrs.at[pl.ds(0, n_blocks)], wrs.at[pl.ds(0, n_blocks)], 8, to_mate).wait_send()

    @pl.when(owner)
    def _():
        gathered(OWNERS - 1)
        copy(wrr.at[pl.ds(0, 31)], wrr.at[pl.ds(0, 31)], 9, to_mate).wait_send()

    @pl.when(jnp.logical_not(owner))
    def _():
        gathered(OWNERS)

    send_e = copy(wfull.at[core], wfull.at[core], 10, to_mate)
    send_e.start()
    copy(wfull.at[1 - core], wfull.at[1 - core], 10, to_mate).wait_recv()
    for half in range(2):
        for side_cols in range(2):
            dw_ref[half * 192 : half * 192 + 192, side_cols * 384 : side_cols * 384 + 384] = (
                wfull[half, side_cols * 12 : side_cols * 12 + 12].reshape(192, 384).astype(F32)
            )

    for sent in (send_g, send_a, send_b, send_c, send_d, send_m, send_w, send_x, send_k, send_f, send_e):
        sent.wait_send()
    copy(x2.at[core, pl.ds(0, 31)], x2.at[core, pl.ds(0, 31)], 4, to_mate).wait_send()
    copy(dxb.at[pl.ds(0, 31)], dxb.at[pl.ds(0, 31)], 12, to_mate).wait_send()


def per_device(queries, keys, values, offsets, w_out, grad_mixed):
    vmem = pl.BlockSpec(memory_space=pltpu.VMEM)
    V = pltpu.VMEM
    block = jax.ShapeDtypeStruct((TOK, 384), BF16)
    scratch = [
        V((4, 3, 256, 128), BF16),
        V((2, CHIPS, 16, 384), BF16),
        V((TOK, 384), BF16),
        V((3, 128, TOK), BF16),
        V((3, 128, TOK), BF16),
        V((3, 128, TOK), BF16),
        V((3, 128, TOK), BF16),
        V((6, 128, 128), BF16),
        V((48, 384), BF16),
        V((6, 128, TOK), BF16),
        V((3, 16, TOK), BF16),
        V((6, TOK, TOK), BF16),
        V((6, TOK, 128), BF16),
        V((48, 1024), F32),
        V((6, HD, TOK), F32),
        V((6, HD, TOK), F32),
        V((48, 384), F32),
        V((6, 8, TOK), F32),
        V((6, 8, TOK), F32),
        V((2, 48, 128), F32),
        V((384, TOK), BF16),
        V((TOK, 384), BF16),
        V((6, 8, TOK), F32),
        V((384, TOK), BF16),
        V((TOK, 384), BF16),
        V((TOK, 384), BF16),
        V((OWNERS, 16, 384), BF16),
        V((OWNERS, 16, 384), F32),
        V((OWNERS, 16, 384), BF16),
        V((OWNERS, 16, 384), BF16),
        V((CHIPS, 16, 384), BF16),
        V((2, OWNERS, 16, 384), BF16),
        V((48, 384), BF16),
        V((48, 128), F32),
        V((2, CHIPS, 16, 384), F32),
        V((CHIPS, 16, 384), BF16),
        V((CHIPS, 16, 384), BF16),
        V((CHIPS, 16, 384), BF16),
        V((CHIPS, 16, 384), BF16),
        V((48, 384), F32),
        V((6, HD, TOK), F32),
        V((4, 3, 256, 128), F32),
        V((2, 3, 256, 128), BF16),
        V((2, 3, 256, 128), BF16),
        V((3, 256, 128), BF16),
        V((3, 256, 128), BF16),
        V((3, TOK, 128), F32),
        V((3, TOK, 128), F32),
        pltpu.SemaphoreType.DMA((15,)),
        pltpu.SemaphoreType.DMA((15,)),
    ]
    return pl.pallas_call(
        kernel,
        out_shape=(block, block, block, block, jax.ShapeDtypeStruct((384, 768), F32)),
        in_specs=[pl.BlockSpec(memory_space=pltpu.SMEM)] + [vmem] * 5,
        out_specs=(vmem,) * 5,
        scratch_shapes=scratch,
        compiler_params=pltpu.CompilerParams(
            collective_id=0, has_side_effects=True, vmem_limit_bytes=60 << 20
        ),
    )(offsets, queries, keys, values, w_out, grad_mixed)


def solution(mesh):
    in_specs = (
        P("seq", "head"),
        P("seq", "head"),
        P("seq", "head"),
        P(),
        P("head", None),
        P("seq", "head"),
    )
    out_specs = (
        P("seq", "head"),
        P("seq", "head"),
        P("seq", "head"),
        P("seq", "head"),
        P("head", None),
    )
    return jax.shard_map(
        per_device, mesh=mesh, in_specs=in_specs, out_specs=out_specs, check_vma=False
    )
```

time: 901 us -> 63.2 us (0.07)
  waiting for transfers between devices: 448 us -> 0 us
  local copies, waits for them, and re-layouts: 152 us -> 6.24 us
  matrix products: 126 us -> 0 us
  blocking collectives: 101 us -> 0 us
  Pallas kernels: 0 us -> 56.1 us
  other arithmetic: 46.9 us -> 0 us
  between operations: 16.7 us -> 0.66 us
    unnamed x3 -> x0, waiting for transfers between devices: 442 us -> none
    dot_general x129 -> x0, matrix products: 126 us -> none  [the longest x18 33.4 us: head_out(): jnp.einsum('qk,kd->qd', weights_bf, value_rows, preferred_element_type=jn...]
    all_gather x2 -> x0, blocking collectives: 101 us -> none  [the longest x1 86.3 us: gather_group(): return (lax.all_gather(pieces[0], 'seq', axis=1, tiled=True),)]
    pallas_call x0 -> x1, Pallas kernels: none -> 56.1 us  [per_device(): pl.pallas_call(kernel, out_shape=(block, block, block, block, jax.ShapeDt...]
    broadcast_in_dim x40 -> x0, local copies, waits for them, and re-layouts: 46.9 us -> none  [put_rows(): spread = jnp.where(hits, source[:, None], jnp.zeros((), source.dtype))]
    another operation x24 -> x0, local copies, waits for them, and re-layouts: 27.9 us -> none  [the longest x8 11.3 us: pick_rows(): source.reshape((source.shape[0] // stride, stride) + source.shape[1:])]
    sub x24 -> x0, local copies, waits for them, and re-layouts: 19.6 us -> none  [the longest x12 11.3 us: head_out(): head_scores(query_rows, key_rows) - lse_rows[:, None]]
    reduce_sum x24 -> x0, other arithmetic: 19.4 us -> none  [the longest x5 13.4 us: pick_rows(): jnp.sum(jnp.where(hits, grouped, jnp.zeros((), source.dtype)), axis=1)]
  transfers between devices with their start and end apart: 6 -> 0, of which waited for: 2 -> 0; matrix products, arithmetic and copies ran while one was open for 16% -> 0% of each run, Pallas kernels for 0% -> 0%
where the time goes in v1:
time: 63.2 us; the launch traced here: 63.1 us
  Pallas kernels  56.1 us (89%)
  local copies, waits for them, and re-layouts  6.24 us (10%)
  between operations  0.66 us (1%)
    pallas_call x1, Pallas kernels, per_device(): pl.pallas_call(kernel, out_shape=(block, block, block, block, jax.ShapeDt...  56.1 us
    unnamed x11, local copies, waits for them, and re-layouts  6.24 us

profile of v1, /device:TPU:1, one launch (start us, length us, event | category | flops | bytes accessed | tf_op | source)
XLA Modules:
  0.0 63.1 jit_solution(12644073922036029111)
XLA Ops:
  0.6 56.1 %shard_map.101 = (bf16[512,384]{1,0:T(8,128)(2,1)}, bf16[512,384]{1,0:T(8,128)(2,1)}, bf16[512,384]{1,0:T(8,128)(2,1)}, bf16[512,384]{1,0:T(8,128)(2,1)}, f32[384,768]{1,0:T(8,128)}) custom-call(s32[2,12]{1,0:T(2,128)} %off_ref.1, bf16[512,384]{1,0:T(8,128)(2,1)} %q_ref.1, bf16[512,384]{1,0:T(8,128)(2,1)} %k_ref.1, bf16[512,384]{1,0:T(8,128)(2,1)} %v_ref.1, ...), custom_call_target="tpu_custom_call" | custom-call | tf_op jit(solution)/shard_map/pallas_call | solution.py:530
  56.8 0.0 copy-start.2
  56.8 0.0 copy-start.1
  56.8 1.9 %copy.16 = bf16[512,384]{1,0:T(8,128)(2,1)} copy(bf16[512,384]{1,0:T(8,128)(2,1)} %get-tuple-element.10) | data formatting | bytes 786432
  58.7 0.0 copy-start
  58.7 1.9 %copy.17 = bf16[512,384]{1,0:T(8,128)(2,1)} copy(bf16[512,384]{1,0:T(8,128)(2,1)} %get-tuple-element.11) | data formatting | bytes 786432
  60.5 0.0 copy-done.2
  60.5 0.7 %copy.18 = bf16[512,384]{1,0:T(8,128)(2,1)} copy(bf16[512,384]{1,0:T(8,128)(2,1)S(1)} %copy-done.2) | data formatting | bytes 786432
  61.3 0.0 copy-done.1
  61.3 0.7 %copy.19 = bf16[512,384]{1,0:T(8,128)(2,1)} copy(bf16[512,384]{1,0:T(8,128)(2,1)S(1)} %copy-done.1) | data formatting | bytes 786432
  62.0 0.0 copy-done
  62.0 1.0 %copy.20 = f32[384,768]{1,0:T(8,128)} copy(f32[384,768]{1,0:T(8,128)S(1)} %copy-done) | data formatting | bytes 2359296
Async XLA Ops:
  56.8 3.8 %copy-start.2 = (bf16[512,384]{1,0:T(8,128)(2,1)S(1)}, bf16[512,384]{1,0:T(8,128)(2,1)}, u32[]{:S(2)}) copy-start(bf16[512,384]{1,0:T(8,128)(2,1)} %get-tuple-element.12) | copy-start | bytes 1179652
  56.8 4.5 %copy-start.1 = (bf16[512,384]{1,0:T(8,128)(2,1)S(1)}, bf16[512,384]{1,0:T(8,128)(2,1)}, u32[]{:S(2)}) copy-start(bf16[512,384]{1,0:T(8,128)(2,1)} %get-tuple-element.13) | copy-start | bytes 1179652
  58.7 3.4 %copy-start = (f32[384,768]{1,0:T(8,128)S(1)}, f32[384,768]{1,0:T(8,128)}, u32[]{:S(2)}) copy-start(f32[384,768]{1,0:T(8,128)} %get-tuple-element.14) | copy-start | bytes 3538948

commit v2 on v1

v2 whole, which is shorter than its diff:
```python
import math

import jax
import jax.numpy as jnp
from jax import lax
from jax.experimental import pallas as pl
from jax.experimental.pallas import tpu as pltpu
from jax.sharding import PartitionSpec as P

HD = 64
TOK = 512
CHIPS = 32
PLANE = 8
ROWS = 4
OWNERS = 6
SCALE = 0.125 * math.log2(math.e)
MESH = pl.DeviceIdType.MESH
F32 = jnp.float32
BF16 = jnp.bfloat16


def nn(a, b):
    return lax.dot_general(a, b, (((1,), (0,)), ((), ())), preferred_element_type=F32)


def nt(a, b):
    return lax.dot_general(a, b, (((1,), (1,)), ((), ())), preferred_element_type=F32)


def tn(a, b):
    return lax.dot_general(a, b, (((0,), (0,)), ((), ())), preferred_element_type=F32)


def iota(shape, dim):
    return lax.broadcasted_iota(jnp.int32, shape, dim)


def halves(x):
    hi = x.astype(BF16)
    return hi, (x - hi.astype(F32)).astype(BF16)


def thirds(x):
    hi = x.astype(BF16).astype(F32)
    mid = (x - hi).astype(BF16).astype(F32)
    return [hi, mid, x - hi - mid]


def kernel(
    off_ref, q_hbm, k_hbm, v_hbm, w_hbm, g_hbm,
    mixed_hbm, dq_hbm, dk_hbm, dv_hbm, dw_hbm,
    q_ref, k_ref, v_ref, w_ref, g_ref, mixed_ref, dq_ref, dk_ref, dv_ref, dw_ref,
    kv1, x2, goth, qt, kt, vt, k1t, q1t, q2, e1, e2, p0, p1, p2, o0, o1, o2,
    m0s, l0s, m1s, l1s, gs, ds, at, an, gt, mxs, mxr, wps, wpo, wmr, wrs, wyr, wy, wxr, wfull,
    do2, dx, dxs, dxm, dxb, xyr, xb, xr, dq2, dqx, dk1, dks, dkm, dkc, dkr,
    ssem, rsem, isem, osem,
):
    s = lax.axis_index("seq")
    h = lax.axis_index("head")
    chip, core = s // 2, lax.rem(s, 2)
    r = lax.rem(s, 4)
    mate = s + 1 - 2 * core
    side = lax.rem(chip, 2)
    facing = s + 2 - 4 * side
    r_mate = r + 1 - 2 * core
    r_facing = r + 2 - 4 * side
    r_other = r_mate + 2 - 4 * side
    first = h * 6
    row, place = chip // PLANE, lax.rem(chip, PLANE)
    owner = place < OWNERS
    own_row = pl.ds(row * PLANE, PLANE)
    to_mate, to_facing, to_half = (mate, h), (facing, h), (s, 1 - h)

    def peer(c):
        return (2 * c + core, h)

    def copy(src, dst, n, device):
        return pltpu.make_async_remote_copy(
            src_ref=src, dst_ref=dst, send_sem=ssem.at[n], recv_sem=rsem.at[n],
            device_id=device, device_id_type=MESH,
        )

    loads = [
        pltpu.make_async_copy(src, dst, isem.at[i])
        for i, (src, dst) in enumerate(
            ((k_hbm, k_ref), (v_hbm, v_ref), (q_hbm, q_ref), (g_hbm, g_ref), (w_hbm, w_ref))
        )
    ]
    for load in loads:
        load.start()

    barrier = pltpu.get_barrier_semaphore()

    in_plane = [peer(row * PLANE + lax.rem(place + i, PLANE)) for i in range(1, PLANE)]
    other_rows = [lax.rem(row + i, ROWS) for i in range(1, ROWS)]
    in_column = [peer(other * PLANE + place) for other in other_rows]
    for device in [to_mate, to_half] + in_plane + in_column:
        pl.semaphore_signal(barrier, inc=1, device_id=device, device_id_type=MESH)

    lane128 = iota((1, 128), 1)
    lane256 = iota((1, 256), 1)
    lane512 = iota((1, TOK), 1)
    row128 = iota((128, 1), 0)
    row16 = iota((16, 1), 0)
    row8 = iota((8, 1), 0)
    pair16 = (row16 < 8) == (lane128 < HD)
    first_lanes = lane256 < 128
    diagonal = (row128 < HD) == first_lanes
    left = lax.rem(lane256, 128) < HD
    PAIRS = range(3)

    def cols(p):
        return slice(p * 128, p * 128 + 128)

    q2[...] = jnp.zeros_like(q2)
    do2[...] = jnp.zeros_like(do2)
    ds[...] = jnp.zeros_like(ds)
    for stat in (m0s, l0s, m1s, l1s):
        stat[...] = jnp.ones_like(stat)
    hits = []
    hits2 = []
    f1 = jnp.zeros((8, 1), jnp.int32)
    f2 = jnp.zeros((8, 1), jnp.int32)
    for n in range(6):
        f1 = jnp.where(row8 == n, off_ref[0, first + n], f1)
        f2 = jnp.where(row8 == n, off_ref[1, first + n], f2)
    rows, columns = iota((128, TOK), 0), iota((128, TOK), 1)
    for p in PAIRS:
        hits.append(
            [
                jnp.where(columns == rows * 4 + off_ref[0, first + 2 * p + j], 1.0, 0.0).astype(BF16)
                for j in range(2)
            ]
        )
        f2p = jnp.where(row16 < 8, off_ref[1, first + 2 * p], off_ref[1, first + 2 * p + 1])
        hits2.append(
            jnp.where(
                iota((16, TOK), 1) == lax.rem(iota((16, TOK), 0), 8) * 64 + f2p, 1.0, 0.0
            ).astype(BF16)
        )
        e1[p, 0:128] = hits[p][0]
        e1[p, 128:256] = hits[p][1]
        e2[p * 16 : p * 16 + 16] = hits2[p]
    loads[0].wait()
    loads[1].wait()
    for p in PAIRS:
        kv = jnp.concatenate([k_ref[:, cols(p)], v_ref[:, cols(p)]], axis=1)
        both = nn(hits2[p], kv)
        few = jnp.where(left, both[0:8], both[8:16])
        x2[core, chip, :, cols(p)] = jnp.concatenate([few[:, 0:128], few[:, 128:256]], axis=0).astype(BF16)
        picked = jnp.where(left, nn(hits[p][0], kv), nn(hits[p][1], kv)).astype(BF16)
        kv1[r, p, 0:128, :] = picked[:, 0:128]
        kv1[r, p, 128:256, :] = picked[:, 128:256]

    pl.semaphore_wait(barrier, PLANE + ROWS)
    send_g = copy(g_hbm, goth, 0, to_half)

    own_block = x2.at[core, chip]
    for device in in_plane:
        copy(own_block, own_block, 4, device).start()
    send_a = copy(kv1.at[r], kv1.at[r], 2, to_facing)
    send_a.start()
    send_b = copy(kv1.at[r], kv1.at[r], 1, to_mate)
    send_b.start()

    send_g.start()
    loads[2].wait()
    for p in PAIRS:
        q = q_ref[:, cols(p)]
        q2[p * 16 : p * 16 + 16, cols(p)] = jnp.where(pair16, nn(hits2[p], q), 0.0).astype(BF16)
        qt[p] = q.T
        kt[p] = k_ref[:, cols(p)].T
        vt[p] = v_ref[:, cols(p)].T
        q1t[p] = jnp.where(diagonal, nt(qt[p], e1[p]), 0.0).astype(BF16)

    def masked(x_t, j):
        mine = (row128 < HD) if j == 0 else (row128 >= HD)
        return jnp.where(mine, x_t, jnp.zeros((), x_t.dtype))

    def near(p):
        k, q_t, v_t = k_ref[:, cols(p)], qt[p], vt[p]
        for j in range(2):
            n = 2 * p + j
            scores = nn(k, masked(q_t, j))
            top = jnp.max(scores, axis=0, keepdims=True)
            weights = jnp.exp2((scores - top) * SCALE).astype(BF16)
            out = nn(
                jnp.concatenate([v_t[HD * j : HD * (j + 1)], jnp.ones((16, TOK), BF16)], axis=0), weights
            )
            p0[n] = weights
            o0[p, HD * j : HD * (j + 1)] = out[0:HD]
            m0s[n : n + 1] = top
            l0s[n : n + 1] = out[HD : HD + 1]

    near(0)
    seven = x2.at[core, pl.ds(0, PLANE - 1)]
    copy(seven, seven, 4, to_mate).wait_recv()
    own_blocks = x2.at[core, own_row]
    for i, device in enumerate(in_column):
        copy(own_blocks, own_blocks, 15 + i, device).start()
    copy(own_blocks, own_blocks, 5, to_mate).start()
    near(1)
    copy(kv1.at[r_facing], kv1.at[r_facing], 2, to_facing).wait_recv()
    send_c = copy(kv1.at[r_facing], kv1.at[r_facing], 3, to_mate)
    send_c.start()
    near(2)
    for i in range(3):
        source = lax.rem(row + ROWS - 1 - i, ROWS)
        arrived = x2.at[core, pl.ds(source * PLANE, PLANE)]
        copy(arrived, arrived, 15 + i, to_mate).wait_recv()
        copy(arrived, arrived, 5, to_mate).start()

    copy(kv1.at[r_mate], kv1.at[r_mate], 1, to_mate).wait_recv()
    copy(kv1.at[r_other], kv1.at[r_other], 3, to_mate).wait_recv()

    keys = [kv1[:, p, 0:128, :].reshape(TOK, 128) for p in PAIRS]
    values = [kv1[:, p, 128:256, :].reshape(TOK, 128) for p in PAIRS]
    scores = [nn(keys[p], q1t[p]) for p in PAIRS]
    v_ts = [values[p].T for p in PAIRS]
    for p in PAIRS:
        k1t[p] = keys[p].T
    tops = [jnp.max(scores[p], axis=0, keepdims=True) for p in PAIRS]
    weights = [jnp.exp2((scores[p] - tops[p]) * SCALE).astype(BF16) for p in PAIRS]
    for p in PAIRS:
        p1[p] = weights[p]
    outs = [
        nn(jnp.concatenate([v_ts[p], jnp.ones((16, TOK), BF16)], axis=0), weights[p]) for p in PAIRS
    ]
    wides = []
    for p in PAIRS:
        hi, lo = halves(jnp.where(diagonal, outs[p][0:128], 0.0))
        stats = []
        for stat in (outs[p][128:129], tops[p]):
            for mine in (first_lanes, jnp.logical_not(first_lanes)):
                stats += thirds(jnp.where(mine, stat, 0.0))
        stats = jnp.concatenate(stats + [jnp.zeros((4, 256), F32)], axis=0).astype(BF16)
        wides.append(nn(jnp.concatenate([hi, lo, stats], axis=0), e1[p]))
    for p in PAIRS:
        wide = wides[p]
        o1[p] = wide[0:128] + wide[128:256]
        for j in range(2):
            n = 2 * p + j
            l1s[n : n + 1] = jnp.sum(wide[256 + 3 * j : 259 + 3 * j], axis=0, keepdims=True)
            m1s[n : n + 1] = jnp.sum(wide[262 + 3 * j : 265 + 3 * j], axis=0, keepdims=True)

    copy(x2.at[1 - core], x2.at[1 - core], 5, to_mate).wait_recv()
    own_head = iota((48, 384), 0) // 8 == iota((48, 384), 1) // HD
    xs = x2[...].reshape(1024, 384)
    scores2 = nt(q2[...], xs)
    scores2 = jnp.where(lax.rem(iota((1, 1024), 1), 16) < 8, scores2, -1e30)
    top2 = jnp.max(scores2, axis=1, keepdims=True)
    weights2 = jnp.exp2((scores2 - top2) * SCALE).astype(BF16).astype(F32)
    p2[...] = weights2
    o2[...] = jnp.where(own_head, nn(pltpu.roll(weights2, 8, 1).astype(BF16), xs), 0.0)
    sum2 = jnp.sum(weights2, axis=1, keepdims=True)

    def expand2(part, hit2):
        hi, lo = halves(part)
        return tn(jnp.concatenate([hi, lo], axis=0), jnp.concatenate([hit2, hit2], axis=0))

    def expand2_right(part, hit2):
        hi, lo = halves(part)
        return tn(jnp.concatenate([hit2, hit2], axis=0), jnp.concatenate([hi, lo], axis=0))

    lane48 = iota((48, 48), 1)
    same_head = iota((48, 48), 0) // 8 == lax.rem(lane48, 8)
    table = jnp.zeros((48, 48), F32)
    for t, piece in enumerate(thirds(top2) + thirds(sum2)):
        table = jnp.where(lane48 // 8 == t, piece, table)
    table = jnp.where(same_head, table, 0.0).astype(BF16)
    stats2 = tn(table, e2[...])
    m2 = stats2[0:8] + stats2[8:16] + stats2[16:24]
    l2 = stats2[24:32] + stats2[32:40] + stats2[40:48]
    m0, l0, l1 = m0s[...], l0s[...], l1s[...]
    m1 = jnp.where(lax.rem(lane512, 4) == f1, m1s[...], -1e30)
    m2 = jnp.where(lax.rem(lane512, 64) == f2, m2, -1e30)
    highest = jnp.maximum(m0, jnp.maximum(m1, m2))
    c0 = jnp.exp2((m0 - highest) * SCALE)
    c1 = jnp.exp2((m1 - highest) * SCALE)
    c2 = jnp.exp2((m2 - highest) * SCALE)
    over = 1.0 / (c0 * l0 + c1 * l1 + c2 * l2)
    g0, g1, g2 = c0 * over, c1 * over, c2 * over
    gs[0] = g0
    gs[1] = g1
    gs[2] = g2
    fars = [expand2(o2[p * 16 : p * 16 + 16, cols(p)], e2[p * 16 : p * 16 + 16]) for p in PAIRS]
    for p in PAIRS:
        found = []
        for j in range(2):
            n = 2 * p + j
            part = slice(HD * j, HD * (j + 1))
            found.append(
                g0[n : n + 1] * o0[p, part] + g1[n : n + 1] * o1[p, part] + g2[n : n + 1] * fars[p][part]
            )
        both = jnp.concatenate(found, axis=0)
        at[p * 128 : p * 128 + 128, :] = both.astype(BF16)
        an[:, cols(p)] = both.T.astype(BF16)

    loads[3].wait()
    loads[4].wait()
    own_cols = pl.ds(pl.multiple_of(h * 384, 128), 384)
    other_cols = pl.ds(pl.multiple_of((1 - h) * 384, 128), 384)
    mxs[...] = nn(an[...], w_ref[:, other_cols]).astype(BF16)
    send_m = copy(mxs, mxr, 6, to_half)
    send_m.start()

    mate_rows = pl.ds(pl.multiple_of((1 - core) * 192, 64), 192)
    own_rows = pl.ds(pl.multiple_of(core * 192, 64), 192)
    wps[pl.ds(h * 12, 12)] = nn(at[mate_rows, :], g_ref[...]).astype(BF16).reshape(12, 16, 384)
    wpo[pl.ds(h * 12, 12)] = nn(at[own_rows, :], g_ref[...]).reshape(12, 16, 384)
    copy(goth, goth, 0, to_half).wait_recv()
    wps[pl.ds((1 - h) * 12, 12)] = nn(at[mate_rows, :], goth[...]).astype(BF16).reshape(12, 16, 384)
    send_w = copy(wps, wmr, 7, to_mate)
    send_w.start()
    gt[...] = (nt(w_ref[:, own_cols], g_ref[...]) + nt(w_ref[:, other_cols], goth[...])).astype(BF16)
    wpo[pl.ds((1 - h) * 12, 12)] = nn(at[own_rows, :], goth[...]).reshape(12, 16, 384)

    for n in range(6):
        own = slice(HD * n, HD * (n + 1))
        ds[n : n + 1] = jnp.sum(
            gt[own, :].astype(F32) * at[own, :].astype(F32), axis=0, keepdims=True
        )
    gs[...] = 0.125 * gs[...]

    def weighted(level, p):
        return jnp.concatenate(
            [
                (gt[HD * n : HD * (n + 1), :].astype(F32) * gs[level, n : n + 1]).astype(BF16)
                for n in (2 * p, 2 * p + 1)
            ],
            axis=0,
        )

    shares2 = gs[2] * ds[...]
    deltas2 = []
    for p in PAIRS:
        sixteen = slice(p * 16, p * 16 + 16)
        do2[sixteen, cols(p)] = jnp.where(pair16, nt(e2[sixteen], weighted(2, p)), 0.0).astype(BF16)
        share = jnp.where(row16 < 8, shares2[2 * p : 2 * p + 1], shares2[2 * p + 1 : 2 * p + 2])
        deltas2.append(jnp.sum(e2[sixteen].astype(F32) * share, axis=1, keepdims=True))
    delta2 = jnp.concatenate(deltas2, axis=0)

    xs = x2[...].reshape(1024, 384)
    weights2 = p2[...]
    grad_prob2 = pltpu.roll(nt(do2[...], xs), 1024 - 8, 1)
    dscore2 = weights2 * (grad_prob2 - delta2)
    left_side = jnp.concatenate([dscore2, 8.0 * pltpu.roll(weights2, 8, 1)], axis=0).astype(BF16)
    dx[...] = tn(left_side, jnp.concatenate([q2[...], do2[...]], axis=0)).reshape(2, CHIPS, 16, 384)
    dxs[...] = dx[1 - core].astype(BF16)
    send_x = copy(dxs, dxm, 11, to_mate)
    send_x.start()
    dq2[...] = jnp.where(own_head, nn(dscore2.astype(BF16), xs), 0.0)

    copy(wmr, wmr, 7, to_mate).wait_recv()
    wrs[...] = (wpo[...] + wmr[...].astype(F32)).astype(BF16)

    for i, device in enumerate(in_column):
        copy(wrs.at[pl.ds(other_rows[i] * OWNERS, OWNERS)], wyr.at[row], 8, device).start()

    fews = []
    for p in PAIRS:
        share = gs[1] * ds[...]
        stats = jnp.concatenate(
            thirds(share[2 * p : 2 * p + 1]) + thirds(share[2 * p + 1 : 2 * p + 2])
            + [jnp.zeros((10, TOK), F32)],
            axis=0,
        ).astype(BF16)
        fews.append(nt(jnp.concatenate([weighted(1, p), stats], axis=0), e1[p]))
    grads = [jnp.where(diagonal, fews[p][0:128], 0.0).astype(BF16) for p in PAIRS]
    deltas = [
        jnp.where(
            first_lanes,
            jnp.sum(fews[p][128:131], axis=0, keepdims=True),
            jnp.sum(fews[p][131:134], axis=0, keepdims=True),
        )
        for p in PAIRS
    ]
    values = [kv1[:, p, 128:256, :].reshape(TOK, 128) for p in PAIRS]
    grad_probs = [nn(values[p], grads[p]) for p in PAIRS]
    dscores = [(p1[p].astype(F32) * (grad_probs[p] - deltas[p])).astype(BF16) for p in PAIRS]
    for p in PAIRS:
        dk1[:, p, 0:128, :] = nt(dscores[p], q1t[p]).reshape(4, 128, 128)
        dk1[:, p, 128:256, :] = (8.0 * nt(p1[p], grads[p])).reshape(4, 128, 128)
    dks[0] = dk1[r_mate].astype(BF16)
    dks[1] = dk1[r_other].astype(BF16)
    send_k = copy(dks, dkm, 13, to_mate)
    send_k.start()

    copy(dxm, dxm, 11, to_mate).wait_recv()
    dxb[...] = (dx[core] + dxm[...].astype(F32)).astype(BF16)

    for i, device in enumerate(in_column):
        copy(dxb.at[pl.ds(other_rows[i] * PLANE, PLANE)], xyr.at[row], 12, device).start()

    wyr[row] = wrs[pl.ds(row * OWNERS, OWNERS)]
    copy(wyr.at[pl.ds(0, 3)], wyr.at[pl.ds(0, 3)], 8, to_mate).wait_recv()
    wy[...] = jnp.sum(wyr[...].astype(F32), axis=0).astype(BF16)
    for k in range(OWNERS):

        @pl.when(place != k)
        def _():
            copy(wy.at[k], wxr.at[place], 18, peer(row * PLANE + k)).start()

    firsts = [nn(k1t[p], dscores[p]) for p in PAIRS]
    for p in PAIRS:
        hi, lo = halves(jnp.where(diagonal, firsts[p], 0.0))
        wide = nn(jnp.concatenate([hi, lo], axis=0), e1[p])
        dqx[p] = wide[0:128] + wide[128:256] + expand2(
            dq2[p * 16 : p * 16 + 16, cols(p)], e2[p * 16 : p * 16 + 16]
        )
    nears = []

    def near_back(p):
        k_t, q_t, v = kt[p], qt[p], v_ref[:, cols(p)]
        grad_k = jnp.zeros((TOK, 128), F32)
        grad_v = jnp.zeros((TOK, 128), F32)
        grad_q = []
        grad = weighted(0, p)
        share = gs[0] * ds[...]
        for j in range(2):
            n = 2 * p + j
            grad_m = masked(grad, j)
            prob = p0[n]
            dscore = (prob.astype(F32) * (nn(v, grad_m) - share[n : n + 1])).astype(BF16)
            grad_q.append(nn(k_t[HD * j : HD * (j + 1)], dscore))
            grad_k = grad_k + nt(dscore, masked(q_t, j))
            grad_v = grad_v + nt(prob, grad_m)
        dq_ref[:, cols(p)] = (jnp.concatenate(grad_q, axis=0) + dqx[p]).T.astype(BF16)
        nears.append((grad_k, 8.0 * grad_v))

    near_back(0)
    copy(dkm, dkm, 13, to_mate).wait_recv()
    dkc[...] = (dk1[r_facing] + dkm[1].astype(F32)).astype(BF16)
    send_f = copy(dkc, dkr, 14, to_facing)
    send_f.start()
    near_back(1)

    xyr[row] = dxb[own_row]
    copy(xyr.at[pl.ds(0, 3)], xyr.at[pl.ds(0, 3)], 12, to_mate).wait_recv()
    xb[...] = jnp.sum(xyr[...].astype(F32), axis=0).astype(BF16)
    for i, device in enumerate(in_plane):
        copy(xb.at[lax.rem(place + 1 + i, PLANE)], xr.at[place], 19, device).start()

    @pl.when(owner)
    def _():
        wxr[place] = wy[place]
        copy(wxr.at[pl.ds(0, 7)], wxr.at[pl.ds(0, 7)], 18, to_mate).wait_recv()
        result = wfull.at[core, row * OWNERS + place]
        result[...] = jnp.sum(wxr[...].astype(F32), axis=0).astype(BF16)
        for device in in_plane:
            copy(result, result, 9, device).start()

    near_back(2)

    def plane_done(n_blocks):
        some = wfull.at[core, pl.ds(0, n_blocks)]
        copy(some, some, 9, to_mate).wait_recv()
        copy(wy.at[pl.ds(0, n_blocks)], wy.at[pl.ds(0, n_blocks)], 18, to_mate).wait_send()

    @pl.when(owner)
    def _():
        plane_done(OWNERS - 1)

    @pl.when(jnp.logical_not(owner))
    def _():
        plane_done(OWNERS)

    own_w = wfull.at[core, pl.ds(row * OWNERS, OWNERS)]
    for i, device in enumerate(in_column):
        copy(own_w, own_w, 20 + i, device).start()
    copy(own_w, own_w, 10, to_mate).start()
    outputs = [
        pltpu.make_async_copy(src, dst, osem.at[i])
        for i, (src, dst) in enumerate(
            (
                (mixed_ref, mixed_hbm), (dq_ref, dq_hbm), (dk_ref, dk_hbm),
                (dv_ref, dv_hbm), (dw_ref, dw_hbm),
            )
        )
    ]
    outputs[1].start()

    own_part = nn(an[...], w_ref[:, own_cols])
    copy(mxr, mxr, 6, to_half).wait_recv()
    mixed_ref[...] = (own_part + mxr[...].astype(F32)).astype(BF16)
    outputs[0].start()

    xr[place] = xb[place]
    copy(xr.at[pl.ds(0, 7)], xr.at[pl.ds(0, 7)], 19, to_mate).wait_recv()
    far = jnp.sum(xr[...].astype(F32), axis=0)
    copy(dkr, dkr, 14, to_facing).wait_recv()
    for p in PAIRS:
        near1 = dk1[r, p] + dkm[0, p].astype(F32) + dkr[p].astype(F32)
        near1 = jnp.concatenate([near1[0:128], near1[128:256]], axis=1)
        near1 = jnp.concatenate([jnp.where(left, near1, 0.0), jnp.where(left, 0.0, near1)], axis=0)
        hi, lo = halves(near1)
        few = jnp.concatenate([far[0:8, cols(p)], far[8:16, cols(p)]], axis=1)
        few = jnp.concatenate([jnp.where(left, few, 0.0), jnp.where(left, 0.0, few)], axis=0)
        total = tn(e1[p], hi) + tn(e1[p], lo) + expand2_right(few, e2[p * 16 : p * 16 + 16])
        dk_ref[:, cols(p)] = (nears[p][0] + total[:, 0:128]).astype(BF16)
        dv_ref[:, cols(p)] = (nears[p][1] + total[:, 128:256]).astype(BF16)
    outputs[2].start()
    outputs[3].start()

    for i in range(3):
        source = lax.rem(row + ROWS - 1 - i, ROWS)
        arrived = wfull.at[core, pl.ds(source * OWNERS, OWNERS)]
        copy(arrived, arrived, 20 + i, to_mate).wait_recv()
        copy(arrived, arrived, 10, to_mate).start()

    def write_w(half):
        for side_cols in range(2):
            dw_ref[pl.ds(pl.multiple_of(half * 192, 64), 192), side_cols * 384 : side_cols * 384 + 384] = wfull[
                half, side_cols * 12 : side_cols * 12 + 12
            ].reshape(192, 384)

    write_w(core)
    copy(wfull.at[1 - core], wfull.at[1 - core], 10, to_mate).wait_recv()
    write_w(1 - core)
    outputs[4].start()

    for sent in (send_g, send_a, send_b, send_c, send_m, send_w, send_x, send_k, send_f):
        sent.wait_send()
    copy(seven, seven, 4, to_mate).wait_send()
    copy(x2.at[core], x2.at[core], 5, to_mate).wait_send()
    for i in range(3):
        copy(own_blocks, own_blocks, 15 + i, to_mate).wait_send()
        copy(own_w, own_w, 20 + i, to_mate).wait_send()
    copy(wyr.at[pl.ds(0, 3)], wyr.at[pl.ds(0, 3)], 8, to_mate).wait_send()
    copy(xyr.at[pl.ds(0, 3)], xyr.at[pl.ds(0, 3)], 12, to_mate).wait_send()
    copy(xr.at[pl.ds(0, 7)], xr.at[pl.ds(0, 7)], 19, to_mate).wait_send()
    copy(wfull.at[core], wfull.at[core], 10, to_mate).wait_send()

    @pl.when(owner)
    def _():
        copy(wxr.at[pl.ds(0, 7)], wxr.at[pl.ds(0, 7)], 9, to_mate).wait_send()

    for output in outputs:
        output.wait()


def deliver(*refs):
    sources, targets, buffers, wide = refs[0:5], refs[5:10], refs[10:15], refs[15]
    in_sems, out_sems = refs[16:18]
    parts = [(i, half) for i in range(5) for half in range(2)]

    def rows(i, half):
        count = sources[i].shape[0] // 2
        return pl.ds(half * count, count)

    ins = [
        pltpu.make_async_copy(sources[i].at[rows(i, k)], buffers[i].at[rows(i, k)], in_sems.at[i, k])
        for i, k in parts
    ]
    for one in ins:
        one.start()
    outs = []
    for (i, k), one in zip(parts, ins):
        one.wait()
        source = buffers[i]
        if i == 4:
            wide[rows(i, k), :] = source[rows(i, k), :].astype(F32)
            source = wide
        outs.append(
            pltpu.make_async_copy(source.at[rows(i, k)], targets[i].at[rows(i, k)], out_sems.at[i, k])
        )
        outs[-1].start()
    for one in outs:
        one.wait()


def per_device(queries, keys, values, offsets, w_out, grad_mixed):
    anywhere = pl.BlockSpec(memory_space=pl.ANY)
    V = pltpu.VMEM
    block = jax.ShapeDtypeStruct((TOK, 384), BF16)
    scratch = [V((TOK, 384), BF16)] * 3 + [V((384, 768), BF16)] + [V((TOK, 384), BF16)] * 5 + [
        V((384, 768), BF16),
        V((4, 3, 256, 128), BF16),
        V((2, CHIPS, 16, 384), BF16),
        V((TOK, 384), BF16),
        V((3, 128, TOK), BF16),
        V((3, 128, TOK), BF16),
        V((3, 128, TOK), BF16),
        V((3, 128, TOK), BF16),
        V((3, 128, 256), BF16),
        V((48, 384), BF16),
        V((3, 256, TOK), BF16),
        V((48, TOK), BF16),
        V((6, TOK, TOK), BF16),
        V((3, TOK, 256), BF16),
        V((48, 1024), F32),
        V((3, 128, TOK), F32),
        V((3, 128, TOK), F32),
        V((48, 384), F32),
        V((8, TOK), F32),
        V((8, TOK), F32),
        V((8, TOK), F32),
        V((8, TOK), F32),
        V((3, 8, TOK), F32),
        V((8, TOK), F32),
        V((384, TOK), BF16),
        V((TOK, 384), BF16),
        V((384, TOK), BF16),
        V((TOK, 384), BF16),
        V((TOK, 384), BF16),
        V((24, 16, 384), BF16),
        V((24, 16, 384), F32),
        V((24, 16, 384), BF16),
        V((24, 16, 384), BF16),
        V((ROWS, OWNERS, 16, 384), BF16),
        V((OWNERS, 16, 384), BF16),
        V((PLANE, 16, 384), BF16),
        V((2, 24, 16, 384), BF16),
        V((48, 384), BF16),
        V((2, CHIPS, 16, 384), F32),
        V((CHIPS, 16, 384), BF16),
        V((CHIPS, 16, 384), BF16),
        V((CHIPS, 16, 384), BF16),
        V((ROWS, PLANE, 16, 384), BF16),
        V((PLANE, 16, 384), BF16),
        V((PLANE, 16, 384), BF16),
        V((48, 384), F32),
        V((3, 128, TOK), F32),
        V((4, 3, 256, 128), F32),
        V((2, 3, 256, 128), BF16),
        V((2, 3, 256, 128), BF16),
        V((3, 256, 128), BF16),
        V((3, 256, 128), BF16),
        pltpu.SemaphoreType.DMA((23,)),
        pltpu.SemaphoreType.DMA((23,)),
        pltpu.SemaphoreType.DMA((5,)),
        pltpu.SemaphoreType.DMA((5,)),
    ]
    results = pl.pallas_call(
        kernel,
        out_shape=(block, block, block, block, jax.ShapeDtypeStruct((384, 768), BF16)),
        in_specs=[pl.BlockSpec(memory_space=pltpu.SMEM)] + [anywhere] * 5,
        out_specs=(anywhere,) * 5,
        scratch_shapes=scratch,
        compiler_params=pltpu.CompilerParams(
            collective_id=0, has_side_effects=True, vmem_limit_bytes=60 << 20
        ),
    )(offsets, queries, keys, values, w_out, grad_mixed)
    return pl.pallas_call(
        deliver,
        out_shape=(block, block, block, block, jax.ShapeDtypeStruct((384, 768), F32)),
        in_specs=[anywhere] * 5,
        out_specs=(anywhere,) * 5,
        scratch_shapes=[V((TOK, 384), BF16)] * 4 + [
            V((384, 768), BF16),
            V((384, 768), F32),
            pltpu.SemaphoreType.DMA((5, 2)),
            pltpu.SemaphoreType.DMA((5, 2)),
        ],
        compiler_params=pltpu.CompilerParams(vmem_limit_bytes=60 << 20),
    )(*results)


def solution(mesh):
    in_specs = (
        P("seq", "head"),
        P("seq", "head"),
        P("seq", "head"),
        P(),
        P("head", None),
        P("seq", "head"),
    )
    out_specs = (
        P("seq", "head"),
        P("seq", "head"),
        P("seq", "head"),
        P("seq", "head"),
        P("head", None),
    )
    return jax.shard_map(
        per_device, mesh=mesh, in_specs=in_specs, out_specs=out_specs, check_vma=False
    )
```

time: 63.2 us -> 51.2 us (0.81)
  local copies, waits for them, and re-layouts: 6.24 us -> 0 us
  Pallas kernels: 56.1 us -> 50.2 us
    pallas_call x1, Pallas kernels: 56.1 us -> 47.4 us  [per_device(): pl.pallas_call(kernel, out_shape=(block, block, block, block, jax.ShapeDt...]
    unnamed x11 -> x0, local copies, waits for them, and re-layouts: 6.24 us -> none
    pallas_call x0 -> x1, Pallas kernels: none -> 2.78 us  [per_device(): pl.pallas_call(deliver, out_shape=(block, block, block, block, jax.ShapeD...]
where the time goes in v2:
time: 51.2 us; the launch traced here: 51 us
  Pallas kernels  50.2 us (98%)
  between operations  0.8 us (2%)
    pallas_call x1, Pallas kernels, per_device(): pl.pallas_call(kernel, out_shape=(block, block, block, block, jax.ShapeDt...  47.4 us
    pallas_call x1, Pallas kernels, per_device(): pl.pallas_call(deliver, out_shape=(block, block, block, block, jax.ShapeD...  2.78 us

profile of v2, /device:TPU:1, one launch (start us, length us, event | category | flops | bytes accessed | tf_op | source)
XLA Modules:
  0.0 51.0 jit_solution(2528081735798581949)
XLA Ops:
  0.6 47.4 %shard_map.101 = (bf16[512,384]{1,0:T(8,128)(2,1)}, bf16[512,384]{1,0:T(8,128)(2,1)}, bf16[512,384]{1,0:T(8,128)(2,1)}, bf16[512,384]{1,0:T(8,128)(2,1)}, bf16[384,768]{1,0:T(8,128)(2,1)}) custom-call(s32[2,12]{1,0:T(2,128)} %off_ref.1, bf16[512,384]{1,0:T(8,128)(2,1)} %q_hbm.1, bf16[512,384]{1,0:T(8,128)(2,1)} %k_hbm.1, bf16[512,384]{1,0:T(8,128)(2,1)} %v_hbm.1, ...), custom_call_target="tpu_custom_call" | custom-call | tf_op jit(solution)/shard_map/pallas_call | solution.py:634
  48.1 2.8 %shard_map.102 = (bf16[512,384]{1,0:T(8,128)(2,1)}, bf16[512,384]{1,0:T(8,128)(2,1)}, bf16[512,384]{1,0:T(8,128)(2,1)}, bf16[512,384]{1,0:T(8,128)(2,1)}, f32[384,768]{1,0:T(8,128)}) custom-call(bf16[512,384]{1,0:T(8,128)(2,1)} %get-tuple-element.10.refs_0_, bf16[512,384]{1,0:T(8,128)(2,1)} %get-tuple-element.11.refs_1_, ...), custom_call_target="tpu_custom_call" | custom-call | tf_op jit(solution)/shard_map/pallas_call | solution.py:644

commit v3 on v2

--- a/solution.py
+++ b/solution.py
@@ -57,22 +57,28 @@
 ):
     s = lax.axis_index("seq")
     h = lax.axis_index("head")
-    chip, core = s // 2, lax.rem(s, 2)
+    seat, core = s // 2, lax.rem(s, 2)
+    x_at, z_at, y_at = lax.rem(seat, 4), lax.rem(seat // 4, 2), seat // 8
     r = lax.rem(s, 4)
     mate = s + 1 - 2 * core
-    side = lax.rem(chip, 2)
+    side = lax.rem(seat, 2)
     facing = s + 2 - 4 * side
     r_mate = r + 1 - 2 * core
     r_facing = r + 2 - 4 * side
     r_other = r_mate + 2 - 4 * side
     first = h * 6
-    row, place = chip // PLANE, lax.rem(chip, PLANE)
+    row = (1 - core) * y_at + core * x_at
+    place = z_at * 4 + (1 - core) * x_at + core * y_at
+    chip = row * PLANE + place
     owner = place < OWNERS
     own_row = pl.ds(row * PLANE, PLANE)
     to_mate, to_facing, to_half = (mate, h), (facing, h), (s, 1 - h)
 
     def peer(c):
-        return (2 * c + core, h)
+        major, deep, minor = c // PLANE, lax.rem(c, PLANE) // 4, lax.rem(c, 4)
+        y_to = (1 - core) * major + core * minor
+        x_to = (1 - core) * minor + core * major
+        return (2 * (y_to * 8 + deep * 4 + x_to) + core, h)
 
     def copy(src, dst, n, device):
         return pltpu.make_async_remote_copy(
@@ -433,14 +439,6 @@
     dkc[...] = (dk1[r_facing] + dkm[1].astype(F32)).astype(BF16)
     send_f = copy(dkc, dkr, 14, to_facing)
     send_f.start()
-    near_back(1)
-
-    xyr[row] = dxb[own_row]
-    copy(xyr.at[pl.ds(0, 3)], xyr.at[pl.ds(0, 3)], 12, to_mate).wait_recv()
-    xb[...] = jnp.sum(xyr[...].astype(F32), axis=0).astype(BF16)
-    for i, device in enumerate(in_plane):
-        copy(xb.at[lax.rem(place + 1 + i, PLANE)], xr.at[place], 19, device).start()
-
     @pl.when(owner)
     def _():
         wxr[place] = wy[place]
@@ -450,7 +448,13 @@
         for device in in_plane:
             copy(result, result, 9, device).start()
 
-    near_back(2)
+    near_back(1)
+
+    xyr[row] = dxb[own_row]
+    copy(xyr.at[pl.ds(0, 3)], xyr.at[pl.ds(0, 3)], 12, to_mate).wait_recv()
+    xb[...] = jnp.sum(xyr[...].astype(F32), axis=0).astype(BF16)
+    for i, device in enumerate(in_plane):
+        copy(xb.at[lax.rem(place + 1 + i, PLANE)], xr.at[place], 19, device).start()
 
     def plane_done(n_blocks):
         some = wfull.at[core, pl.ds(0, n_blocks)]
@@ -469,6 +473,8 @@
     for i, device in enumerate(in_column):
         copy(own_w, own_w, 20 + i, device).start()
     copy(own_w, own_w, 10, to_mate).start()
+    near_back(2)
+
     outputs = [
         pltpu.make_async_copy(src, dst, osem.at[i])
         for i, (src, dst) in enumerate(

time: 51.2 us -> 48.4 us (0.945)
  Pallas kernels: 50.2 us -> 47.4 us
    pallas_call x1, Pallas kernels: 47.4 us -> 44.6 us  [per_device(): pl.pallas_call(kernel, out_shape=(block, block, block, block, jax.ShapeDt...]
where the time goes in v3:
time: 48.4 us; the launch traced here: 48.2 us
  Pallas kernels  47.4 us (98%)
  between operations  0.8 us (2%)
    pallas_call x1, Pallas kernels, per_device(): pl.pallas_call(kernel, out_shape=(block, block, block, block, jax.ShapeDt...  44.6 us
    pallas_call x1, Pallas kernels, per_device(): pl.pallas_call(deliver, out_shape=(block, block, block, block, jax.ShapeD...  2.78 us

profile of v3, /device:TPU:1, one launch (start us, length us, event | category | flops | bytes accessed | tf_op | source)
XLA Modules:
  0.0 48.2 jit_solution(16987859616351668483)
XLA Ops:
  0.6 44.6 %shard_map.101 = (bf16[512,384]{1,0:T(8,128)(2,1)}, bf16[512,384]{1,0:T(8,128)(2,1)}, bf16[512,384]{1,0:T(8,128)(2,1)}, bf16[512,384]{1,0:T(8,128)(2,1)}, bf16[384,768]{1,0:T(8,128)(2,1)}) custom-call(s32[2,12]{1,0:T(2,128)} %off_ref.1, bf16[512,384]{1,0:T(8,128)(2,1)} %q_hbm.1, bf16[512,384]{1,0:T(8,128)(2,1)} %k_hbm.1, bf16[512,384]{1,0:T(8,128)(2,1)} %v_hbm.1, ...), custom_call_target="tpu_custom_call" | custom-call | tf_op jit(solution)/shard_map/pallas_call | solution.py:640
  45.3 2.8 %shard_map.102 = (bf16[512,384]{1,0:T(8,128)(2,1)}, bf16[512,384]{1,0:T(8,128)(2,1)}, bf16[512,384]{1,0:T(8,128)(2,1)}, bf16[512,384]{1,0:T(8,128)(2,1)}, f32[384,768]{1,0:T(8,128)}) custom-call(bf16[512,384]{1,0:T(8,128)(2,1)} %get-tuple-element.10.refs_0_, bf16[512,384]{1,0:T(8,128)(2,1)} %get-tuple-element.11.refs_1_, ...), custom_call_target="tpu_custom_call" | custom-call | tf_op jit(solution)/shard_map/pallas_call | solution.py:650

commit v4 on v3

--- a/solution.py
+++ b/solution.py
@@ -314,10 +314,13 @@
     own_rows = pl.ds(pl.multiple_of(core * 192, 64), 192)
     wps[pl.ds(h * 12, 12)] = nn(at[mate_rows, :], g_ref[...]).astype(BF16).reshape(12, 16, 384)
     wpo[pl.ds(h * 12, 12)] = nn(at[own_rows, :], g_ref[...]).reshape(12, 16, 384)
+    early_w = wps.at[pl.ds(h * 12, 12)]
+    copy(early_w, wmr.at[pl.ds(h * 12, 12)], 7, to_mate).start()
     copy(goth, goth, 0, to_half).wait_recv()
     wps[pl.ds((1 - h) * 12, 12)] = nn(at[mate_rows, :], goth[...]).astype(BF16).reshape(12, 16, 384)
     send_w = copy(wps, wmr, 7, to_mate)
-    send_w.start()
+    late_w = wps.at[pl.ds((1 - h) * 12, 12)]
+    copy(late_w, wmr.at[pl.ds((1 - h) * 12, 12)], 7, to_mate).start()
     gt[...] = (nt(w_ref[:, own_cols], g_ref[...]) + nt(w_ref[:, other_cols], goth[...])).astype(BF16)
     wpo[pl.ds((1 - h) * 12, 12)] = nn(at[own_rows, :], goth[...]).reshape(12, 16, 384)
 
@@ -390,7 +393,6 @@
     dks[0] = dk1[r_mate].astype(BF16)
     dks[1] = dk1[r_other].astype(BF16)
     send_k = copy(dks, dkm, 13, to_mate)
-    send_k.start()
 
     copy(dxm, dxm, 11, to_mate).wait_recv()
     dxb[...] = (dx[core] + dxm[...].astype(F32)).astype(BF16)
@@ -398,6 +400,7 @@
     for i, device in enumerate(in_column):
         copy(dxb.at[pl.ds(other_rows[i] * PLANE, PLANE)], xyr.at[row], 12, device).start()
 
+    send_k.start()
     wyr[row] = wrs[pl.ds(row * OWNERS, OWNERS)]
     copy(wyr.at[pl.ds(0, 3)], wyr.at[pl.ds(0, 3)], 8, to_mate).wait_recv()
     wy[...] = jnp.sum(wyr[...].astype(F32), axis=0).astype(BF16)

time: 48.4 us -> 48.4 us (level)
  no operation moved by 1% of the time
where the time goes in v4:
time: 48.4 us; the launch traced here: 48.2 us
  Pallas kernels  47.4 us (98%)
  between operations  0.8 us (2%)
    pallas_call x1, Pallas kernels, per_device(): pl.pallas_call(kernel, out_shape=(block, block, block, block, jax.ShapeDt...  44.6 us
    pallas_call x1, Pallas kernels, per_device(): pl.pallas_call(deliver, out_shape=(block, block, block, block, jax.ShapeD...  2.78 us

profile of v4, /device:TPU:1, one launch (start us, length us, event | category | flops | bytes accessed | tf_op | source)
XLA Modules:
  0.0 48.2 jit_solution(6209804262424887409)
XLA Ops:
  0.6 44.6 %shard_map.101 = (bf16[512,384]{1,0:T(8,128)(2,1)}, bf16[512,384]{1,0:T(8,128)(2,1)}, bf16[512,384]{1,0:T(8,128)(2,1)}, bf16[512,384]{1,0:T(8,128)(2,1)}, bf16[384,768]{1,0:T(8,128)(2,1)}) custom-call(s32[2,12]{1,0:T(2,128)} %off_ref.1, bf16[512,384]{1,0:T(8,128)(2,1)} %q_hbm.1, bf16[512,384]{1,0:T(8,128)(2,1)} %k_hbm.1, bf16[512,384]{1,0:T(8,128)(2,1)} %v_hbm.1, ...), custom_call_target="tpu_custom_call" | custom-call | tf_op jit(solution)/shard_map/pallas_call | solution.py:643
  45.3 2.8 %shard_map.102 = (bf16[512,384]{1,0:T(8,128)(2,1)}, bf16[512,384]{1,0:T(8,128)(2,1)}, bf16[512,384]{1,0:T(8,128)(2,1)}, bf16[512,384]{1,0:T(8,128)(2,1)}, f32[384,768]{1,0:T(8,128)}) custom-call(bf16[512,384]{1,0:T(8,128)(2,1)} %get-tuple-element.10.refs_0_, bf16[512,384]{1,0:T(8,128)(2,1)} %get-tuple-element.11.refs_1_, ...), custom_call_target="tpu_custom_call" | custom-call | tf_op jit(solution)/shard_map/pallas_call | solution.py:653
